TPU v7x, 512 devices: a whole 4x4x16 slice. The times are simulated.
512 devices in a mesh: row: 16 (over z), col: 32 (over y, x, core).
Axes of the slice: x: 4, y: 4, z: 16, core: 2. Of those that a mesh axis runs over, the one named last changes fastest.
Arguments:
- tokens: bfloat16 [2048, 8192], P('col', 'row'), may hold values from -6 to 6
- cotangent: bfloat16 [2048, 8192], P('col', 'row'), may hold values from -42.33202 to 42.33202
- gate_pre: bfloat16 [2048, 14336], P('row', 'col'), may hold values from -6 to 6
- up_act: bfloat16 [2048, 14336], P('row', 'col'), may hold values from -6 to 6
- gate_weight: bfloat16 [8192, 14336], P('row', 'col'), may hold values from -6 to 6
- up_weight: bfloat16 [8192, 14336], P('row', 'col'), may hold values from -6 to 6
- down_weight: bfloat16 [14336, 8192], P('col', 'row'), may hold values from -9 to 9
- moment_m: bfloat16 [14336, 8192], P('col', 'row'), may hold values from -6 to 6
- moment_v: bfloat16 [14336, 8192], P('col', 'row'), may hold values from 0.1 to 1.6015625
Outputs:
- grad_input: bfloat16 [2048, 8192], P('col', 'row')
- grad_gate: bfloat16 [8192, 14336], P('row', 'col')
- grad_up: bfloat16 [8192, 14336], P('row', 'col')
- new_m: bfloat16 [14336, 8192], P('col', 'row')
- new_v: bfloat16 [14336, 8192], P('col', 'row')
- step_down: bfloat16 [14336, 8192], P('col', 'row')
- trust_ratio: float32 [], replicated
All inputs are finite; a program needn't handle non-finite values.
Results may differ from a plain program's by a relative error of at most 0.03.
Values may be sent and summed in bfloat16 or wider, within the bound.
No kernel may reach another device: no remote copies, remote signals or barrier semaphores. Data moves between devices by JAX's collectives and lax.ppermute only.
A program may use at most 64 MiB of HBM per device.

v0:
```python
import functools

import jax
import jax.numpy as jnp
from jax import lax
from jax.experimental import pallas as pl
from jax.experimental.pallas import tpu as pltpu
from jax.sharding import PartitionSpec as P

D = 8192
FF = 14336
Z = 16
SIDE = 4
CHIPS = 16
COLS = 32
SCALE_WIDTH = float(D) ** (-0.5)
SCALE_HIDDEN = float(FF) ** (-0.5)
BF16 = jnp.bfloat16
F32 = jnp.float32
VMEM = pl.BlockSpec(memory_space=pltpu.VMEM)
SMEM = pl.BlockSpec(memory_space=pltpu.SMEM)
HBM = pl.BlockSpec(memory_space=pltpu.HBM)
DMA = pltpu.SemaphoreType.DMA


def params(mebibytes=20):
    return pltpu.CompilerParams(vmem_limit_bytes=mebibytes * 1024 * 1024)


def shift_z(v, step):
    pairs = []
    for z in range(Z):
        for col in range(COLS):
            way = step if col % 2 == 0 else -step
            pairs.append((z * COLS + col, (z + way) % Z * COLS + col))
    return lax.ppermute(v, ("row", "col"), pairs)


def swap_core(v):
    return lax.ppermute(v, "col", [(c, c ^ 1) for c in range(COLS)])


def exchange_chips(v):
    groups = [[2 * chip + core for chip in range(CHIPS)] for core in range(2)]
    return lax.all_to_all(v, "col", 0, 0, axis_index_groups=groups, tiled=True)


def gather_chips(v):
    mine = exchange_chips(jnp.broadcast_to(v[None], (CHIPS, *v.shape)))
    return mine, swap_core(mine)


def add(*terms):
    total = terms[0].astype(F32)
    for term in terms[1:]:
        total = total + term.astype(F32)
    return total.astype(BF16)


def reduce_z(zero, far, odd, even, give_odd, give_even, beside):
    own = shift_z(odd, 1)
    got_odd = swap_core(give_odd)
    their = shift_z(got_odd, 1)
    far = shift_z(far, SIDE)
    got_even = swap_core(give_even)
    moving_their = add(got_even[2], their[3])
    moving = add(even[2], own[3])
    done = []
    for k in (2, 1, 0):
        moving_their = shift_z(moving_their, 2)
        moving = shift_z(moving, 2)
        moving, ready = lax.optimization_barrier((moving, beside[2 - k]))
        done.append(ready)
        if k == 2:
            moving = add(moving, even[1], own[2], far)
        elif k == 1:
            moving = add(moving, even[0], own[1])
        if k > 0:
            moving_their = add(moving_their, got_even[k - 1], their[k])
    extra = done[2]
    other = jnp.concatenate([add(moving_their, their[0]), jnp.zeros_like(extra)], axis=0)
    mine = jnp.concatenate([add(zero, moving, own[0]), extra], axis=0)
    got_mine = swap_core(other)
    got_other = swap_core(mine)
    return add(mine, got_mine), add(other, got_other), done


GROUPS = ((0, -2, -4, -6), (2, 4, 6), (-1, -3, -5, -7), (1, 3, 5, 7, -8))


def owner_of(place_ref, offset):
    z, way = place_ref[0], place_ref[2]
    return lax.rem(z + way * offset + Z, Z)


def hidden_partial_body(place_ref, mine_ref, other_ref, weight_ref, cot_ref, *refs):
    zero_ref, far_ref, odd_ref, even_ref, give_odd_ref, give_even_ref, hold = refs
    core = place_ref[1]
    chips, rows, _ = mine_ref.shape
    for chip in range(chips):
        own = pl.multiple_of(chip * 2 * rows + core * rows, rows)
        their = pl.multiple_of(chip * 2 * rows + (1 - core) * rows, rows)
        cot_ref[pl.ds(own, rows), :] = mine_ref[chip]
        cot_ref[pl.ds(their, rows), :] = other_ref[chip]
    tokens = cot_ref.shape[0]
    width = tokens // Z
    span = tokens // SIDE
    for part in range(SIDE):
        product = lax.dot_general(
            weight_ref[...],
            cot_ref[part * span : (part + 1) * span, :],
            (((1,), (1,)), ((), ())),
            preferred_element_type=F32,
        )
        hold[:, part * span : (part + 1) * span] = (product * SCALE_HIDDEN).astype(BF16)

    def block(offset):
        low = pl.multiple_of(owner_of(place_ref, offset) * width, width)
        return hold[:, pl.ds(low, width)]

    zero_ref[...] = block(0)
    far_ref[...] = block(8)
    for k, offset in enumerate((1, 3, 5, 7)):
        odd_ref[k] = block(offset)
        give_odd_ref[k] = block(-offset)
    for k, offset in enumerate((2, 4, 6)):
        even_ref[k] = block(offset)
        give_even_ref[k] = block(-offset)


def hidden_partial(place, mine, other, weight):
    units, depth = weight.shape
    tokens = mine.shape[0] * mine.shape[1] * 2
    width = tokens // Z
    shapes = [(tokens, depth), (units, width), (units, width)]
    shapes += [(count, units, width) for count in (4, 3, 4, 3)]
    return pl.pallas_call(
        hidden_partial_body,
        out_shape=[jax.ShapeDtypeStruct(shape, BF16) for shape in shapes],
        in_specs=[SMEM] + [VMEM] * 3,
        out_specs=[VMEM] * 7,
        scratch_shapes=[pltpu.VMEM((units, tokens), BF16)],
        compiler_params=params(),
        cost_estimate=pl.CostEstimate(
            flops=2 * units * depth * tokens,
            bytes_accessed=2 * (2 * tokens * depth + units * depth + units * tokens),
            transcendentals=0,
        ),
        name="hidden_partial",
    )(place, mine, other, weight)


def start(source, target, sem):
    copy = pltpu.make_async_copy(source, target, sem)
    copy.start()
    return copy


def activations_body(acts_hbm, *refs):
    outs, (acts_ref, swish_ref, slope_ref, hidden_ref, in_sems, out_sems) = refs[:3], refs[3:]
    blocks, units, width = acts_ref.shape
    units = units // 2
    chunk = 64
    arriving = [start(acts_hbm.at[k], acts_ref.at[k], in_sems.at[k]) for k in range(blocks)]
    leaving = []
    for k in range(blocks):
        cols = slice(k * width, (k + 1) * width)
        arriving[k].wait()

        @pl.loop(0, units // chunk)
        def _(i, k=k, cols=cols):
            low = pl.multiple_of(i * chunk, chunk)
            rows = pl.ds(low, chunk)
            g = acts_ref[k, rows, :].astype(F32)
            u = acts_ref[k, pl.ds(low + units, chunk), :].astype(F32)
            s = jax.nn.sigmoid(g)
            swish = g * s
            slope = u * s * (1.0 + g * (1.0 - s))
            hidden_ref[rows, cols] = (swish * u).astype(BF16)
            swish_ref[rows, cols] = swish.astype(BF16)
            slope_ref[rows, cols] = slope.astype(BF16)

        if k % 4 == 3:
            part = slice((k - 3) * width, (k + 1) * width)
            for n, ref in enumerate((swish_ref, slope_ref, hidden_ref)):
                leaving.append(
                    start(ref.at[:, part], outs[n].at[:, part], out_sems.at[n, k // 4])
                )
    for copy in leaving:
        copy.wait()


def activations(acts):
    blocks, units, width = acts.shape
    units, tokens = units // 2, blocks * width
    return pl.pallas_call(
        activations_body,
        out_shape=[jax.ShapeDtypeStruct((units, tokens), BF16)] * 3,
        in_specs=[HBM],
        out_specs=[HBM] * 3,
        scratch_shapes=[pltpu.VMEM(acts.shape, BF16)]
        + [pltpu.VMEM((units, tokens), BF16)] * 3
        + [DMA((blocks,)), DMA((3, blocks // 4))],
        compiler_params=params(56),
        cost_estimate=pl.CostEstimate(
            flops=30 * units * tokens,
            bytes_accessed=10 * units * tokens,
            transcendentals=units * tokens,
        ),
        name="activations",
    )(acts)


def down_body(hidden_hbm, cot_hbm, weight_hbm, m_hbm, v_hbm, *refs):
    outs, sums_ref = refs[:3], refs[3]
    hidden_ref, cot_ref, weight_ref, m_ref, v_ref = refs[4:9]
    new_m_ref, new_v_ref, update_ref, product, sems, out_sems = refs[9:]
    units = weight_ref.shape[0]
    span = cot_ref.shape[0] // SIDE
    parts = [slice(k * span, (k + 1) * span) for k in range(SIDE)]
    arriving = []
    for k, part in enumerate(parts):
        arriving.append(
            (
                start(hidden_hbm.at[:, part], hidden_ref.at[:, part], sems.at[0, k]),
                start(cot_hbm.at[part], cot_ref.at[part], sems.at[1, k]),
            )
        )
    moments = [
        start(weight_hbm, weight_ref, sems.at[2, 0]),
        start(m_hbm, m_ref, sems.at[2, 1]),
        start(v_hbm, v_ref, sems.at[2, 2]),
    ]
    for k, part in enumerate(parts):
        for copy in arriving[k]:
            copy.wait()
        term = lax.dot_general(
            hidden_ref[:, part],
            cot_ref[part, :],
            (((1,), (0,)), ((), ())),
            preferred_element_type=F32,
        )
        product[...] = term if k == 0 else product[...] + term
    for copy in moments:
        copy.wait()
    step = 16
    depth = product.shape[1]

    def optimizer(i, carry):
        weight_sum, update_sum = carry
        rows = pl.ds(pl.multiple_of(i * step, step), step)
        grad = product[rows, :] * SCALE_HIDDEN
        weight = weight_ref[rows, :].astype(F32)
        first = 0.9 * m_ref[rows, :].astype(F32) + 0.1 * grad
        second = 0.95 * v_ref[rows, :].astype(F32) + 0.05 * grad * grad
        update = first / (jnp.sqrt(second) + 1e-08) + 0.1 * weight
        new_m_ref[rows, :] = first.astype(BF16)
        new_v_ref[rows, :] = second.astype(BF16)
        update_ref[rows, :] = update
        return weight_sum + weight * weight, update_sum + update * update

    zero = jnp.zeros((step, depth), F32)
    weight_sum, update_sum = lax.fori_loop(0, units // step, optimizer, (zero, zero))
    leaving = [
        start(ref, outs[n], out_sems.at[n]) for n, ref in enumerate((new_m_ref, new_v_ref, update_ref))
    ]
    weight_sum = jnp.sum(weight_sum, axis=0, keepdims=True)
    update_sum = jnp.sum(update_sum, axis=0, keepdims=True)
    lanes = sums_ref.shape[1]
    parts = [slice(k, k + lanes) for k in range(0, depth, lanes)]
    weight_sum = sum(weight_sum[:, part] for part in parts)
    update_sum = sum(update_sum[:, part] for part in parts)
    sums_ref[...] = in_rows(weight_sum, update_sum)
    for copy in leaving:
        copy.wait()


def in_rows(first, second):
    row = lax.broadcasted_iota(jnp.int32, (16, first.shape[1]), 0)
    value = jnp.where((row & 1) == 0, first, second)
    high = value.astype(BF16).astype(F32)
    middle = (value - high).astype(BF16).astype(F32)
    low = value - high - middle
    rest = jnp.where(row < 4, middle, jnp.where(row < 6, low, 0.0))
    return jnp.where(row < 2, high, rest).astype(BF16)


def from_rows(rows):
    first = rows[0:1] + rows[2:3] + rows[4:5]
    second = rows[1:2] + rows[3:4] + rows[5:6]
    return jnp.sum(first, axis=1, keepdims=True), jnp.sum(second, axis=1, keepdims=True)


def down_update(hidden, cotangent, weight, moment_m, moment_v):
    units, tokens = hidden.shape
    depth = cotangent.shape[1]
    shapes = [
        jax.ShapeDtypeStruct((units, depth), BF16),
        jax.ShapeDtypeStruct((units, depth), BF16),
        jax.ShapeDtypeStruct((units, depth), F32),
        jax.ShapeDtypeStruct((16, 128), BF16),
    ]
    return pl.pallas_call(
        down_body,
        out_shape=shapes,
        in_specs=[HBM] * 5,
        out_specs=[HBM] * 3 + [VMEM],
        scratch_shapes=[pltpu.VMEM((units, tokens), BF16), pltpu.VMEM((tokens, depth), BF16)]
        + [pltpu.VMEM((units, depth), BF16)] * 5
        + [pltpu.VMEM((units, depth), F32)] * 2
        + [DMA((3, SIDE)), DMA((3,))],
        compiler_params=params(56),
        cost_estimate=pl.CostEstimate(
            flops=2 * units * depth * tokens,
            bytes_accessed=2 * units * tokens + 2 * tokens * depth + 14 * units * depth,
            transcendentals=0,
        ),
        name="down_update",
    )(hidden, cotangent, weight, moment_m, moment_v)


def group_body(number, count, place_ref, *refs):
    grads = refs[:count]
    swish_ref, slope_ref, gate_weight_ref, up_weight_ref = refs[count : count + 4]
    befores = refs[count + 4 : -6]
    gateact_ref, upact_ref, mine_ref, other_ref, sums_ref, hold = refs[-6:]
    units = gateact_ref.shape[0]
    blocks, half, _ = mine_ref.shape
    width = 2 * half
    chunk = 64
    core = place_ref[1]

    def block(k, rows):
        if k == 4:
            return grads[1][rows, :].astype(F32)
        return grads[0][k, rows, :].astype(F32)

    sums = befores[0][...] if befores else 0.0
    for k in range(blocks):
        sums = sums + block(k, slice(units, units + 16))
    sums_ref[...] = sums
    for k, offset in enumerate(GROUPS[number]):
        start = pl.multiple_of(owner_of(place_ref, offset) * width, width)
        cols = slice(k * width, (k + 1) * width)

        @pl.loop(0, units // chunk)
        def _(i, k=k, start=start, cols=cols):
            rows = pl.ds(pl.multiple_of(i * chunk, chunk), chunk)
            grad = block(k, rows)
            swish = swish_ref[rows, pl.ds(start, width)].astype(F32)
            slope = slope_ref[rows, pl.ds(start, width)].astype(F32)
            upact_ref[rows, cols] = (grad * swish).astype(BF16)
            gateact_ref[rows, cols] = (grad * slope).astype(BF16)

    contract_first = (((0,), (0,)), ((), ()))
    product = lax.dot_general(
        gateact_ref[...], gate_weight_ref[...], contract_first, preferred_element_type=F32
    )
    product = product + lax.dot_general(
        upact_ref[...], up_weight_ref[...], contract_first, preferred_element_type=F32
    )
    hold[...] = (product * SCALE_WIDTH).astype(BF16)
    for k in range(blocks):
        own = pl.multiple_of(k * width + core * half, half)
        their = pl.multiple_of(k * width + (1 - core) * half, half)
        mine_ref[k] = hold[pl.ds(own, half), :]
        low = other_ref.shape[0] - (blocks - k) * half - (16 if number == 3 else 0)
        other_ref[low : low + half, :] = hold[pl.ds(their, half), :]
    if number == 3:
        other_ref[blocks * half :, :] = jnp.zeros((16, other_ref.shape[1]), BF16)
        first = sums[0:1] + sums[2:3] + sums[4:5]
        second = sums[1:2] + sums[3:4] + sums[5:6]
        other_ref[blocks * half :, 0:128] = in_rows(first, second)
    elif number > 0:
        earlier = befores[1].shape[0]
        other_ref[0:earlier, :] = befores[1][...]


def input_group(number, place, grads, swish, slope, gate_weight, up_weight, *befores):
    units, tokens = swish.shape
    depth = gate_weight.shape[1]
    width = tokens // Z
    blocks = len(GROUPS[number])
    half = jax.ShapeDtypeStruct((blocks, width // 2, depth), BF16)
    if number == 3:
        other_rows = blocks * width // 2 + 16
    else:
        other_rows = sum(len(offsets) for offsets in GROUPS[: number + 1]) * width // 2
    other = jax.ShapeDtypeStruct((other_rows, depth), BF16)
    acts = jax.ShapeDtypeStruct((units, blocks * width), BF16)
    sums = jax.ShapeDtypeStruct((16, 128), F32)
    return pl.pallas_call(
        functools.partial(group_body, number, len(grads)),
        out_shape=[acts, acts, half, other, sums],
        in_specs=[SMEM] + [VMEM] * (4 + len(grads) + len(befores)),
        out_specs=[VMEM] * 5,
        scratch_shapes=[pltpu.VMEM((blocks * width, depth), BF16)],
        compiler_params=params(),
        cost_estimate=pl.CostEstimate(
            flops=4 * units * depth * blocks * width,
            bytes_accessed=10 * units * blocks * width + 4 * units * depth,
            transcendentals=0,
        ),
        name="input_group",
    )(place, *grads, swish, slope, gate_weight, up_weight, *befores)


def merge_body(place_ref, *refs):
    mine = refs[:SIDE]
    first_other_ref, last_other_ref, sums_ref, out_ref = refs[SIDE:]
    rows, depth = mine[0].shape[1:]
    parts = [(q * rows, slice(q * 128, (q + 1) * 128)) for q in range(depth // 128)]
    for number, offsets in enumerate(GROUPS):
        for k, offset in enumerate(offsets):
            chip = owner_of(place_ref, offset)
            for low, cols in parts:
                out_ref[chip, low : low + rows, :] = mine[number][k, :, cols]
    first = [offset for offsets in GROUPS[:3] for offset in offsets]
    for ref, offsets in ((first_other_ref, first), (last_other_ref, GROUPS[3])):
        for k, offset in enumerate(offsets):
            chip = owner_of(place_ref, -offset)
            for low, cols in parts:
                total = out_ref[chip, low : low + rows, :].astype(F32)
                total = total + ref[k * rows : (k + 1) * rows, cols].astype(F32)
                out_ref[chip, low : low + rows, :] = total.astype(BF16)
    their = last_other_ref[len(GROUPS[3]) * rows :, 0:128].astype(F32)
    first, second = from_rows(sums_ref[...] + their)
    sums = in_rows(jnp.broadcast_to(first, (1, 128)), jnp.broadcast_to(second, (1, 128)))
    for chip in range(out_ref.shape[0]):
        out_ref[chip, len(parts) * rows :, :] = sums


def merge_cores(place, mine, first_other, last_other, sums):
    _, rows, depth = mine[0].shape
    return pl.pallas_call(
        merge_body,
        out_shape=jax.ShapeDtypeStruct((CHIPS, rows * depth // 128 + 16, 128), BF16),
        in_specs=[SMEM] + [VMEM] * (SIDE + 3),
        out_specs=VMEM,
        compiler_params=params(),
        cost_estimate=pl.CostEstimate(
            flops=CHIPS * rows * depth, bytes_accessed=6 * CHIPS * rows * depth, transcendentals=0
        ),
        name="merge_cores",
    )(place, *mine, first_other, last_other, sums)


def finish_body(arrived_ref, update_hbm, grad_input_ref, step_ref, ratio_ref, update_ref, sem):
    copy = start(update_hbm, update_ref, sem)
    chips = arrived_ref.shape[0]
    rows, depth = grad_input_ref.shape
    for q in range(depth // 128):
        for low in range(0, rows, 32):
            part = slice(q * rows + low, q * rows + low + 32)
            total = arrived_ref[0, part, :].astype(F32)
            for chip in range(1, chips):
                total = total + arrived_ref[chip, part, :].astype(F32)
            grad_input_ref[low : low + 32, q * 128 : (q + 1) * 128] = total.astype(BF16)
    part = slice(rows * depth // 128, rows * depth // 128 + 16)
    sums = arrived_ref[0, part, :].astype(F32)
    for chip in range(1, chips):
        sums = sums + arrived_ref[chip, part, :].astype(F32)
    weight_total = sums[0:1] + sums[2:3] + sums[4:5]
    update_total = sums[1:2] + sums[3:4] + sums[5:6]
    ratio = jnp.sqrt(weight_total) / jnp.sqrt(update_total + 1e-06)
    ratio_ref[...] = ratio
    ratio = ratio[:, 0:1]
    step = 16
    copy.wait()

    @pl.loop(0, update_ref.shape[0] // step)
    def _(i):
        part = pl.ds(pl.multiple_of(i * step, step), step)
        step_ref[part, :] = (ratio * update_ref[part, :]).astype(BF16)


def finish(arrived, update):
    chips, rows, _ = arrived.shape
    units, depth = update.shape
    return pl.pallas_call(
        finish_body,
        out_shape=[
            jax.ShapeDtypeStruct(((rows - 16) * 128 // depth, depth), BF16),
            jax.ShapeDtypeStruct((units, depth), BF16),
            jax.ShapeDtypeStruct((1, 128), F32),
        ],
        in_specs=[VMEM, HBM],
        out_specs=[VMEM] * 3,
        scratch_shapes=[pltpu.VMEM((units, depth), F32), DMA],
        compiler_params=params(),
        cost_estimate=pl.CostEstimate(
            flops=chips * rows * 128,
            bytes_accessed=2 * chips * rows * 128 + 6 * units * depth,
            transcendentals=0,
        ),
        name="finish",
    )(arrived, update)


def weight_grads_body(place_ref, *refs):
    gateacts, upacts = refs[:SIDE], refs[SIDE : 2 * SIDE]
    mine_ref, other_ref, grad_gate_ref, grad_up_ref, tokens, act = refs[2 * SIDE :]
    core = place_ref[1]
    chips, half, _ = mine_ref.shape
    width = 2 * half
    for chip in range(chips):
        own = pl.multiple_of(chip * width + core * half, half)
        their = pl.multiple_of(chip * width + (1 - core) * half, half)
        tokens[pl.ds(own, half), :] = mine_ref[chip]
        tokens[pl.ds(their, half), :] = other_ref[chip]
    for acts, out_ref in ((gateacts, grad_gate_ref), (upacts, grad_up_ref)):
        for number, offsets in enumerate(GROUPS):
            for k, offset in enumerate(offsets):
                start = pl.multiple_of(owner_of(place_ref, offset) * width, width)
                act[:, pl.ds(start, width)] = acts[number][:, k * width : (k + 1) * width]
        product = lax.dot_general(
            act[...], tokens[...], (((1,), (0,)), ((), ())), preferred_element_type=F32
        )
        out_ref[...] = (product * SCALE_WIDTH).astype(BF16)


def weight_grads(place, gateacts, upacts, mine, other):
    chips, half, depth = mine.shape
    units = gateacts[0].shape[0]
    tokens = chips * half * 2
    out = jax.ShapeDtypeStruct((units, depth), BF16)
    return pl.pallas_call(
        weight_grads_body,
        out_shape=[out, out],
        in_specs=[SMEM] + [VMEM] * (2 * SIDE + 2),
        out_specs=[VMEM] * 2,
        scratch_shapes=[pltpu.VMEM((tokens, depth), BF16), pltpu.VMEM((units, tokens), BF16)],
        compiler_params=params(),
        cost_estimate=pl.CostEstimate(
            flops=4 * units * depth * tokens,
            bytes_accessed=4 * units * tokens + 2 * tokens * depth + 4 * units * depth,
            transcendentals=0,
        ),
        name="weight_grads",
    )(place, *gateacts, *upacts, mine, other)


def shards(
    tokens, cotangent, gate_pre, up_act, gate_weight, up_weight, down_weight, moment_m, moment_v
):
    z = lax.axis_index("row")
    core = lax.axis_index("col") & 1
    place = jnp.stack([z, core, 1 - 2 * core]).astype(jnp.int32)

    acts = jnp.concatenate([gate_pre.T, up_act.T], axis=0)
    acts, cotangent = lax.optimization_barrier((acts, cotangent))
    acts = lax.all_gather(acts, "row", axis=0, tiled=False)
    cot_mine, cot_other = gather_chips(cotangent)
    cotangent_all, zero, far, odd, even, give_odd, give_even = hidden_partial(
        place, cot_mine, cot_other, down_weight
    )
    tokens, _ = lax.optimization_barrier((tokens, cot_other))
    tok_mine, tok_other = gather_chips(tokens)
    swish, slope, hidden = activations(acts)
    new_m, new_v, update, sums = down_update(
        hidden, cotangent_all, down_weight, moment_m, moment_v
    )
    own, other, (tok_other, swish, _) = reduce_z(
        zero, far, odd, even, give_odd, give_even, (tok_other, swish, sums)
    )

    gate_weight, up_weight = gate_weight.T, up_weight.T

    def group(number, grads, *befores):
        return input_group(
            number, place, grads, swish, slope, gate_weight, up_weight, *befores
        )

    others, owns = [other], [own]
    for _ in range(3):
        others.append(shift_z(others[-1], 2))
        owns.append(shift_z(owns[-1], 2))
    even_other, even = jnp.stack(others), jnp.stack(owns)
    odd_other = shift_z(even_other, 1)
    odd = shift_z(even, 1)
    far = shift_z(owns[3], 2)
    ahead_even = swap_core(even_other[1:])
    group_0 = group(0, (even,))
    group_1 = group(1, (ahead_even,), group_0[4], group_0[3])
    odd_other, odd, far, group_0, group_1 = lax.optimization_barrier(
        (odd_other, odd, far, group_0, group_1)
    )
    ahead_odd = swap_core(odd_other)
    group_2 = group(2, (odd,), group_1[4], group_1[3])
    group_3 = group(3, (ahead_odd, far), group_2[4])
    gateacts, upacts, mine, _, _ = zip(group_0, group_1, group_2, group_3)
    merged = merge_cores(
        place, mine, swap_core(group_2[3]), swap_core(group_3[3]), group_3[4]
    )
    merged, tok_mine = lax.optimization_barrier((merged, tok_mine))
    arrived = exchange_chips(merged)
    grad_gate, grad_up = weight_grads(place, gateacts, upacts, tok_mine, tok_other)
    arrived, grad_gate, grad_up = lax.optimization_barrier((arrived, grad_gate, grad_up))
    grad_input, step_down, ratio = finish(arrived, update)
    return grad_input, grad_gate.T, grad_up.T, new_m, new_v, step_down, ratio[0, 0]


def solution(mesh):
    in_specs = (
        P("col", "row"),
        P("col", "row"),
        P("row", "col"),
        P("row", "col"),
        P("row", "col"),
        P("row", "col"),
        P("col", "row"),
        P("col", "row"),
        P("col", "row"),
    )
    out_specs = (
        P("col", "row"),
        P("row", "col"),
        P("row", "col"),
        P("col", "row"),
        P("col", "row"),
        P("col", "row"),
        P(),
    )
    return jax.shard_map(shards, mesh=mesh, in_specs=in_specs, out_specs=out_specs, check_vma=False)
```

profile of v0, /device:TPU:1, one launch (start us, length us, event | category | flops | bytes accessed | tf_op | source)
XLA Modules:
  0.0 230.9 jit_solution(16216130181922366871)
XLA Ops:
  7.2 1.7 pad_maximum_fusion.3
  8.9 1.0 broadcast_in_dim.4
  9.9 22.8 %all_to_all.15.mine_ref = bf16[16,64,512]{2,1,0:T(8,128)(2,1)S(1)} all-to-all(bf16[16,64,512]{2,1,0:T(8,128)(2,1)S(1)} %broadcast_in_dim.4), channel_id=1, replica_groups={{0,2,4,6,8,10,12,14,16,18,20,22,24,26,28,30},{1,3,5,7,9,11,13,15,17,19,..., dimensions={0} | all-to-all | bytes 2097152 | tf_op jit(solution)/shard_map/all_to_all | solution.py:45
  32.7 5.0 %collective-permute-start = (bf16[16,64,512]{2,1,0:T(8,128)(2,1)S(1)}, bf16[16,64,512]{2,1,0:T(8,128)(2,1)S(1)}, u32[]{:S(2)}, u32[]{:S(2)}) collective-permute-start(bf16[16,64,512]{2,1,0:T(8,128)(2,1)S(1)} %all_to_all.15.mine_ref), channel_id=1, source_target_pairs={{0,1},{1,0},{2,3},{3,2},{4,5},{5,4},{6,7},{7,6},{8,9},{9,8},{10,11... | collective-permute-start | bytes 3145736 | tf_op jit(solution)/shard_map/ppermute | solution.py:40
  37.7 2.3 collective-permute-done.other_ref
  39.9 1.1 broadcast_in_dim.5
  41.2 3.7 %all-to-all-start.1 = ((bf16[16,64,512]{2,1,0:T(8,128)(2,1)}), bf16[16,64,512]{2,1,0:T(8,128)(2,1)S(1)}, u32[]{:S(2)}, u32[]{:S(2)}) async-start(bf16[16,64,512]{2,1,0:T(8,128)(2,1)} %broadcast_in_dim.5), calls=%async_computation.1 | async-start | bytes 2097152 | tf_op jit(solution)/shard_map/all_to_all | solution.py:45
  45.0 1.2 copy-done.10
  46.2 2.3 hidden_partial.1
  48.5 1.4 copy-done.4
  51.3 2.3 collective-permute-start.2
  53.6 1.6 collective-permute-done.2
  55.1 10.8 %collective-permute-start.3 = (bf16[4,448,128]{2,1,0:T(8,128)(2,1)}, bf16[4,448,128]{2,1,0:T(8,128)(2,1)S(1)}, u32[]{:S(2)}, u32[]{:S(2)}) collective-permute-start(bf16[4,448,128]{2,1,0:T(8,128)(2,1)} %collective-permute-done.2), channel_id=1, source_target_pairs={{0,32},{1,481},{2,34},{3,483},{4,36},{5,485},{6,38},{7,487},{8,40}... | collective-permute-start | bytes 1376264 | tf_op jit(solution)/shard_map/ppermute | solution.py:36
  66.0 1.9 collective-permute-start.9
  67.9 2.4 %collective-permute-start.1 = (bf16[3,448,128]{2,1,0:T(8,128)(2,1)}, bf16[3,448,128]{2,1,0:T(8,128)(2,1)S(1)}, u32[]{:S(2)}, u32[]{:S(2)}) collective-permute-start(bf16[3,448,128]{2,1,0:T(8,128)(2,1)} %copy-done.25), channel_id=1, source_target_pairs={{0,1},{1,0},{2,3},{3,2},{4,5},{5,4},{6,7},{7,6},{8,9},{9,8},{10,11... | collective-permute-start | bytes 1032200 | tf_op jit(solution)/shard_map/ppermute | solution.py:40
  70.3 8.0 %collective-permute-start.7 = (bf16[4,448,128]{2,1,0:T(8,128)(2,1)S(1)}, bf16[4,448,128]{2,1,0:T(8,128)(2,1)S(1)}, u32[]{:S(2)}, u32[]{:S(2)}) collective-permute-start(bf16[4,448,128]{2,1,0:T(8,128)(2,1)S(1)} %get-tuple-element.76), channel_id=1, source_target_pairs={{0,32},{1,481},{2,34},{3,483},{4,36},{5,485},{6,38},{7,487},{8,40}... | collective-permute-start | bytes 1376264 | tf_op jit(solution)/shard_map/ppermute | solution.py:36
  78.3 5.2 %collective-permute-start.10 = (bf16[448,128]{1,0:T(8,128)(2,1)}, bf16[448,128]{1,0:T(8,128)(2,1)S(1)}, u32[]{:S(2)}, u32[]{:S(2)}) collective-permute-start(bf16[448,128]{1,0:T(8,128)(2,1)} %copy-done.26), channel_id=1, source_target_pairs={{0,128},{1,385},{2,130},{3,387},{4,132},{5,389},{6,134},{7,391},{8... | collective-permute-start | bytes 344072 | tf_op jit(solution)/shard_map/ppermute | solution.py:36
  83.6 3.1 %collective-permute-start.4 = (bf16[448,128]{1,0:T(8,128)(2,1)S(1)}, bf16[448,128]{1,0:T(8,128)(2,1)S(1)}, u32[]{:S(2)}, u32[]{:S(2)}) collective-permute-start(bf16[448,128]{1,0:T(8,128)(2,1)S(1)} %fusion.7), channel_id=1, source_target_pairs={{0,64},{1,449},{2,66},{3,451},{4,68},{5,453},{6,70},{7,455},{8,72}... | collective-permute-start | bytes 344072 | tf_op jit(solution)/shard_map/ppermute | solution.py:36
  86.7 8.6 %collective-permute-done.7 = bf16[4,448,128]{2,1,0:T(8,128)(2,1)S(1)} collective-permute-done((bf16[4,448,128]{2,1,0:T(8,128)(2,1)S(1)}, bf16[4,448,128]{2,1,0:T(8,128)(2,1)S(1)}, u32[]{:S(2)}, u32[]{:S(2)}) %collective-permute-start.7) | collective-permute-done | bytes 458784 | tf_op jit(solution)/shard_map/ppermute | solution.py:36
  95.4 1.9 collective-permute-start.8
  97.3 1.6 collective-permute-done.4
  99.0 6.0 %collective-permute-start.5 = (bf16[448,128]{1,0:T(8,128)(2,1)S(1)}, bf16[448,128]{1,0:T(8,128)(2,1)S(1)}, u32[]{:S(2)}, u32[]{:S(2)}) collective-permute-start(bf16[448,128]{1,0:T(8,128)(2,1)S(1)} %fusion.6), channel_id=1, source_target_pairs={{0,64},{1,449},{2,66},{3,451},{4,68},{5,453},{6,70},{7,455},{8,72}... | collective-permute-start | bytes 344072 | tf_op jit(solution)/shard_map/ppermute | solution.py:36
  105.0 1.0 copy-done.7
  106.1 1.9 collective-permute-start.11
  108.1 5.6 %collective-permute-start.6 = (bf16[448,128]{1,0:T(8,128)(2,1)S(1)}, bf16[448,128]{1,0:T(8,128)(2,1)S(1)}, u32[]{:S(2)}, u32[]{:S(2)}) collective-permute-start(bf16[448,128]{1,0:T(8,128)(2,1)S(1)} %fusion.5), channel_id=1, source_target_pairs={{0,64},{1,449},{2,66},{3,451},{4,68},{5,453},{6,70},{7,455},{8,72}... | collective-permute-start | bytes 344072 | tf_op jit(solution)/shard_map/ppermute | solution.py:36
  113.7 5.3 %activations.1 = (bf16[448,2048]{1,0:T(8,128)(2,1)}, bf16[448,2048]{1,0:T(8,128)(2,1)}, bf16[448,2048]{1,0:T(8,128)(2,1)}) custom-call(bf16[16,896,128]{2,1,0:T(8,128)(2,1)} %bitcast.78), custom_call_target="tpu_custom_call" | custom-call | flops 27525120 | bytes 9175040 | tf_op jit(solution)/shard_map/activations/pallas_call | solution.py:196
  119.1 2.5 %collective-permute-start.12 = (bf16[448,128]{1,0:T(8,128)(2,1)S(1)}, bf16[448,128]{1,0:T(8,128)(2,1)S(1)}, u32[]{:S(2)}, u32[]{:S(2)}) collective-permute-start(bf16[448,128]{1,0:T(8,128)(2,1)S(1)} %fusion.1), channel_id=1, source_target_pairs={{0,64},{1,449},{2,66},{3,451},{4,68},{5,453},{6,70},{7,455},{8,72}... | collective-permute-start | bytes 344072 | tf_op jit(solution)/shard_map/ppermute | solution.py:36
  121.6 2.3 collective-permute-start.18
  123.9 5.7 %down_update.1 = (bf16[448,512]{1,0:T(8,128)(2,1)}, bf16[448,512]{1,0:T(8,128)(2,1)}, f32[448,512]{1,0:T(8,128)}, bf16[16,128]{1,0:T(8,128)(2,1)}) custom-call(bf16[448,2048]{1,0:T(8,128)(2,1)} %get-tuple-element.83.hidden_hbm, bf16[2048,512]{1,0:T(8,128)(2,1)} %copy-done.4, bf16[448,512]{1,0:T(8,128)(2,1)} %weight_hbm.1, bf16[448,512]{1,0:T(8,128)(2,1)} %m_hbm.1, ...), custom_call_target="tpu_custom_call" | custom-call | flops 939524096 | bytes 7143424 | tf_op jit(solution)/shard_map/down_update/pallas_call | solution.py:303
  129.8 0.8 pad_maximum_fusion.4
  130.6 2.1 collective-permute-start.13
  133.5 4.1 %collective-permute-start.19 = (bf16[464,128]{1,0:T(8,128)(2,1)S(1)}, bf16[464,128]{1,0:T(8,128)(2,1)S(1)}, u32[]{:S(2)}, u32[]{:S(2)}) collective-permute-start(bf16[464,128]{1,0:T(8,128)(2,1)S(1)} %add_convert_fusion), channel_id=1, source_target_pairs={{0,64},{1,449},{2,66},{3,451},{4,68},{5,453},{6,70},{7,455},{8,72}... | collective-permute-start | bytes 356360 | tf_op jit(solution)/shard_map/ppermute | solution.py:36
  137.6 4.4 %collective-permute-start.14 = (bf16[464,128]{1,0:T(8,128)(2,1)S(1)}, bf16[464,128]{1,0:T(8,128)(2,1)S(1)}, u32[]{:S(2)}, u32[]{:S(2)}) collective-permute-start(bf16[464,128]{1,0:T(8,128)(2,1)S(1)} %add_convert_fusion.1), channel_id=1, source_target_pairs={{0,64},{1,449},{2,66},{3,451},{4,68},{5,453},{6,70},{7,455},{8,72}... | collective-permute-start | bytes 356360 | tf_op jit(solution)/shard_map/ppermute | solution.py:36
  142.0 3.5 %collective-permute-start.20 = (bf16[464,128]{1,0:T(8,128)(2,1)S(1)}, bf16[464,128]{1,0:T(8,128)(2,1)S(1)}, u32[]{:S(2)}, u32[]{:S(2)}) collective-permute-start(bf16[464,128]{1,0:T(8,128)(2,1)S(1)} %collective-permute-done.19), channel_id=1, source_target_pairs={{0,64},{1,449},{2,66},{3,451},{4,68},{5,453},{6,70},{7,455},{8,72}... | collective-permute-start | bytes 356360 | tf_op jit(solution)/shard_map/ppermute | solution.py:36
  145.5 4.2 %collective-permute-start.15 = (bf16[464,128]{1,0:T(8,128)(2,1)S(1)}, bf16[464,128]{1,0:T(8,128)(2,1)S(1)}, u32[]{:S(2)}, u32[]{:S(2)}) collective-permute-start(bf16[464,128]{1,0:T(8,128)(2,1)S(1)} %collective-permute-done.14), channel_id=1, source_target_pairs={{0,64},{1,449},{2,66},{3,451},{4,68},{5,453},{6,70},{7,455},{8,72}... | collective-permute-start | bytes 356360 | tf_op jit(solution)/shard_map/ppermute | solution.py:36
  150.1 3.1 %collective-permute-start.21 = (bf16[464,128]{1,0:T(8,128)(2,1)S(1)}, bf16[464,128]{1,0:T(8,128)(2,1)S(1)}, u32[]{:S(2)}, u32[]{:S(2)}) collective-permute-start(bf16[464,128]{1,0:T(8,128)(2,1)S(1)} %collective-permute-done.20), channel_id=1, source_target_pairs={{0,64},{1,449},{2,66},{3,451},{4,68},{5,453},{6,70},{7,455},{8,72}... | collective-permute-start | bytes 356360 | tf_op jit(solution)/shard_map/ppermute | solution.py:36
  153.2 4.3 %collective-permute-start.16 = (bf16[464,128]{1,0:T(8,128)(2,1)S(1)}, bf16[464,128]{1,0:T(8,128)(2,1)S(1)}, u32[]{:S(2)}, u32[]{:S(2)}) collective-permute-start(bf16[464,128]{1,0:T(8,128)(2,1)S(1)} %collective-permute-done.15), channel_id=1, source_target_pairs={{0,64},{1,449},{2,66},{3,451},{4,68},{5,453},{6,70},{7,455},{8,72}... | collective-permute-start | bytes 356360 | tf_op jit(solution)/shard_map/ppermute | solution.py:36
  157.5 1.2 collective-permute-done.21
  158.7 6.4 %collective-permute-start.22 = (bf16[4,464,128]{2,1,0:T(8,128)(2,1)S(1)}, bf16[4,464,128]{2,1,0:T(8,128)(2,1)S(1)}, u32[]{:S(2)}, u32[]{:S(2)}) collective-permute-start(bf16[4,464,128]{2,1,0:T(8,128)(2,1)S(1)} %pad_maximum_fusion.1.refs_0_), channel_id=1, source_target_pairs={{0,32},{1,481},{2,34},{3,483},{4,36},{5,485},{6,38},{7,487},{8,40}... | collective-permute-start | bytes 1425416 | tf_op jit(solution)/shard_map/ppermute | solution.py:36
  165.2 1.9 collective-permute-start.17
  167.2 5.5 %collective-permute-start.24 = (bf16[3,464,128]{2,1,0:T(8,128)(2,1)S(1)}, bf16[3,464,128]{2,1,0:T(8,128)(2,1)S(1)}, u32[]{:S(2)}, u32[]{:S(2)}) collective-permute-start(bf16[3,464,128]{2,1,0:T(8,128)(2,1)S(1)} %pad_maximum_fusion.2), channel_id=1, source_target_pairs={{0,1},{1,0},{2,3},{3,2},{4,5},{5,4},{6,7},{7,6},{8,9},{9,8},{10,11... | collective-permute-start | bytes 1069064 | tf_op jit(solution)/shard_map/ppermute | solution.py:40
  172.7 2.5 %collective-permute-start.23 = (bf16[464,128]{1,0:T(8,128)(2,1)S(1)}, bf16[464,128]{1,0:T(8,128)(2,1)S(1)}, u32[]{:S(2)}, u32[]{:S(2)}) collective-permute-start(bf16[464,128]{1,0:T(8,128)(2,1)S(1)} %collective-permute-done.21), channel_id=1, source_target_pairs={{0,64},{1,449},{2,66},{3,451},{4,68},{5,453},{6,70},{7,455},{8,72}... | collective-permute-start | bytes 356360 | tf_op jit(solution)/shard_map/ppermute | solution.py:36
  175.3 1.8 input_group.4
  177.1 1.5 input_group.5
  179.7 4.0 %collective-permute-start.25 = (bf16[4,464,128]{2,1,0:T(8,128)(2,1)S(1)}, bf16[4,464,128]{2,1,0:T(8,128)(2,1)S(1)}, u32[]{:S(2)}, u32[]{:S(2)}) collective-permute-start(bf16[4,464,128]{2,1,0:T(8,128)(2,1)S(1)} %collective-permute-done.17), channel_id=1, source_target_pairs={{0,1},{1,0},{2,3},{3,2},{4,5},{5,4},{6,7},{7,6},{8,9},{9,8},{10,11... | collective-permute-start | bytes 1425416 | tf_op jit(solution)/shard_map/ppermute | solution.py:40
  183.8 1.8 input_group.6
  187.1 1.9 collective-permute-start.26
  189.0 2.0 input_group.7
  191.9 0.8 copy-done.13
  192.7 2.4 %collective-permute-start.27 = (bf16[336,512]{1,0:T(8,128)(2,1)S(1)}, bf16[336,512]{1,0:T(8,128)(2,1)S(1)}, u32[]{:S(2)}, u32[]{:S(2)}) collective-permute-start(bf16[336,512]{1,0:T(8,128)(2,1)S(1)} %get-tuple-element.111), channel_id=1, source_target_pairs={{0,1},{1,0},{2,3},{3,2},{4,5},{5,4},{6,7},{7,6},{8,9},{9,8},{10,11... | collective-permute-start | bytes 1032200 | tf_op jit(solution)/shard_map/ppermute | solution.py:40
  195.1 1.2 collective-permute-done.27.refs_5_
  196.3 2.0 merge_cores.1
  198.4 6.4 %all-to-all-start.2 = ((bf16[16,272,128]{2,1,0:T(8,128)(2,1)}), bf16[16,272,128]{2,1,0:T(8,128)(2,1)S(1)}, u32[]{:S(2)}, u32[]{:S(2)}) async-start(bf16[16,272,128]{2,1,0:T(8,128)(2,1)} %merge_cores.1), calls=%async_computation.2 | async-start | bytes 2228224 | tf_op jit(solution)/shard_map/all_to_all | solution.py:45
  204.8 1.2 copy-done.8
  206.0 1.1 copy-done.12
  207.1 1.1 copy-done.14
  208.1 1.0 copy-done.16
  209.1 1.0 copy-done.18
  210.1 1.0 copy-done.20
  211.2 1.0 copy-done.22
  212.1 1.0 copy-done.24
  213.1 4.5 %weight_grads.1 = (bf16[448,512]{1,0:T(8,128)(2,1)}, bf16[448,512]{1,0:T(8,128)(2,1)}) custom-call(s32[3]{0:T(128)S(1)} %pad_add_fusion.place_ref, bf16[448,512]{1,0:T(8,128)(2,1)S(1)} %get-tuple-element.114.refs_0_, bf16[448,384]{1,0:T(8,128)(2,1)S(1)} %copy-done.22, bf16[448,512]{1,0:T(8,128)(2,1)S(1)} %copy-done.18, bf16[448,640]{1,0:T(8,128)(2,1)S(1)} %copy-done.12, ...), custom_call_target="tpu_custom_call" | custom-call | flops 1879048192 | bytes 6684672 | tf_op jit(solution)/shard_map/weight_grads/pallas_call | solution.py:527
  217.6 4.2 %all-to-all-done.2.arrived_ref = bf16[16,272,128]{2,1,0:T(8,128)(2,1)S(1)} async-done(((bf16[16,272,128]{2,1,0:T(8,128)(2,1)}), bf16[16,272,128]{2,1,0:T(8,128)(2,1)S(1)}, u32[]{:S(2)}, u32[]{:S(2)}) %all-to-all-start.2) | async-done | bytes 1114144 | tf_op jit(solution)/shard_map/all_to_all | solution.py:45
  221.8 2.2 finish.1
  (85 shorter events, 6.9 us)
Async XLA Ops:
  7.2 106.5 %all-gather.3.cloned.1.call-start = ((), (), s32[]{:S(2)}) async-start(), calls=%async_computation.3 | async-start | bytes 3899392 | tf_op jit(solution)/shard_map/all_gather | solution.py:552
  8.9 31.1 %copy-start.27 = (bf16[64,512]{1,0:T(8,128)(2,1)S(1)}, bf16[64,512]{1,0:T(8,128)(2,1)}, u32[]{:S(2)}) copy-start(bf16[64,512]{1,0:T(8,128)(2,1)} %param.9) | copy-start | bytes 196612
  32.7 12.3 %copy-start.6 = (bf16[448,512]{1,0:T(8,128)(2,1)S(1)}, bf16[448,512]{1,0:T(8,128)(2,1)}, u32[]{:S(2)}) copy-start(bf16[448,512]{1,0:T(8,128)(2,1)} %weight_hbm.1) | copy-start | bytes 1376260
  32.7 7.2 %collective-permute-start = (bf16[16,64,512]{2,1,0:T(8,128)(2,1)S(1)}, bf16[16,64,512]{2,1,0:T(8,128)(2,1)S(1)}, u32[]{:S(2)}, u32[]{:S(2)}) collective-permute-start(bf16[16,64,512]{2,1,0:T(8,128)(2,1)S(1)} %all_to_all.15.mine_ref), channel_id=1, source_target_pairs={{0,1},{1,0},{2,3},{3,2},{4,5},{5,4},{6,7},{7,6},{8,9},{9,8},{10,11... | collective-permute-start | bytes 3145736 | tf_op jit(solution)/shard_map/ppermute | solution.py:40
  39.9 1.3 copy-start.9
  41.2 24.7 %all-to-all-start.1 = ((bf16[16,64,512]{2,1,0:T(8,128)(2,1)}), bf16[16,64,512]{2,1,0:T(8,128)(2,1)S(1)}, u32[]{:S(2)}, u32[]{:S(2)}) async-start(bf16[16,64,512]{2,1,0:T(8,128)(2,1)} %broadcast_in_dim.5), calls=%async_computation.1 | async-start | bytes 2097152 | tf_op jit(solution)/shard_map/all_to_all | solution.py:45
  45.0 1.2 copy-start.10
  48.5 1.4 copy-start.4
  49.9 0.7 copy-start.25
  50.7 0.6 copy-start.26
  51.3 3.8 %collective-permute-start.2 = (bf16[4,448,128]{2,1,0:T(8,128)(2,1)S(1)}, bf16[4,448,128]{2,1,0:T(8,128)(2,1)}, u32[]{:S(2)}, u32[]{:S(2)}) collective-permute-start(bf16[4,448,128]{2,1,0:T(8,128)(2,1)S(1)} %get-tuple-element.73), channel_id=1, source_target_pairs={{0,1},{1,0},{2,3},{3,2},{4,5},{5,4},{6,7},{7,6},{8,9},{9,8},{10,11... | collective-permute-start | bytes 1376264 | tf_op jit(solution)/shard_map/ppermute | solution.py:40
  55.1 28.4 %collective-permute-start.3 = (bf16[4,448,128]{2,1,0:T(8,128)(2,1)}, bf16[4,448,128]{2,1,0:T(8,128)(2,1)S(1)}, u32[]{:S(2)}, u32[]{:S(2)}) collective-permute-start(bf16[4,448,128]{2,1,0:T(8,128)(2,1)} %collective-permute-done.2), channel_id=1, source_target_pairs={{0,32},{1,481},{2,34},{3,483},{4,36},{5,485},{6,38},{7,487},{8,40}... | collective-permute-start | bytes 1376264 | tf_op jit(solution)/shard_map/ppermute | solution.py:36
  66.0 39.0 %collective-permute-start.9 = (bf16[16,64,512]{2,1,0:T(8,128)(2,1)S(1)}, bf16[16,64,512]{2,1,0:T(8,128)(2,1)S(1)}, u32[]{:S(2)}, u32[]{:S(2)}) collective-permute-start(bf16[16,64,512]{2,1,0:T(8,128)(2,1)S(1)} %all-to-all-done.1.refs_8_), channel_id=1, source_target_pairs={{0,1},{1,0},{2,3},{3,2},{4,5},{5,4},{6,7},{7,6},{8,9},{9,8},{10,11... | collective-permute-start | bytes 3145736 | tf_op jit(solution)/shard_map/ppermute | solution.py:40
  67.9 15.6 %collective-permute-start.1 = (bf16[3,448,128]{2,1,0:T(8,128)(2,1)}, bf16[3,448,128]{2,1,0:T(8,128)(2,1)S(1)}, u32[]{:S(2)}, u32[]{:S(2)}) collective-permute-start(bf16[3,448,128]{2,1,0:T(8,128)(2,1)} %copy-done.25), channel_id=1, source_target_pairs={{0,1},{1,0},{2,3},{3,2},{4,5},{5,4},{6,7},{7,6},{8,9},{9,8},{10,11... | collective-permute-start | bytes 1032200 | tf_op jit(solution)/shard_map/ppermute | solution.py:40
  70.3 25.0 %collective-permute-start.7 = (bf16[4,448,128]{2,1,0:T(8,128)(2,1)S(1)}, bf16[4,448,128]{2,1,0:T(8,128)(2,1)S(1)}, u32[]{:S(2)}, u32[]{:S(2)}) collective-permute-start(bf16[4,448,128]{2,1,0:T(8,128)(2,1)S(1)} %get-tuple-element.76), channel_id=1, source_target_pairs={{0,32},{1,481},{2,34},{3,483},{4,36},{5,485},{6,38},{7,487},{8,40}... | collective-permute-start | bytes 1376264 | tf_op jit(solution)/shard_map/ppermute | solution.py:36
  78.3 27.7 %collective-permute-start.10 = (bf16[448,128]{1,0:T(8,128)(2,1)}, bf16[448,128]{1,0:T(8,128)(2,1)S(1)}, u32[]{:S(2)}, u32[]{:S(2)}) collective-permute-start(bf16[448,128]{1,0:T(8,128)(2,1)} %copy-done.26), channel_id=1, source_target_pairs={{0,128},{1,385},{2,130},{3,387},{4,132},{5,389},{6,134},{7,391},{8... | collective-permute-start | bytes 344072 | tf_op jit(solution)/shard_map/ppermute | solution.py:36
  83.6 15.4 %collective-permute-start.4 = (bf16[448,128]{1,0:T(8,128)(2,1)S(1)}, bf16[448,128]{1,0:T(8,128)(2,1)S(1)}, u32[]{:S(2)}, u32[]{:S(2)}) collective-permute-start(bf16[448,128]{1,0:T(8,128)(2,1)S(1)} %fusion.7), channel_id=1, source_target_pairs={{0,64},{1,449},{2,66},{3,451},{4,68},{5,453},{6,70},{7,455},{8,72}... | collective-permute-start | bytes 344072 | tf_op jit(solution)/shard_map/ppermute | solution.py:36
  95.4 9.6 %collective-permute-start.8 = (bf16[448,128]{1,0:T(8,128)(2,1)S(1)}, bf16[448,128]{1,0:T(8,128)(2,1)S(1)}, u32[]{:S(2)}, u32[]{:S(2)}) collective-permute-start(bf16[448,128]{1,0:T(8,128)(2,1)S(1)} %fusion.8), channel_id=1, source_target_pairs={{0,64},{1,449},{2,66},{3,451},{4,68},{5,453},{6,70},{7,455},{8,72}... | collective-permute-start | bytes 344072 | tf_op jit(solution)/shard_map/ppermute | solution.py:36
  99.0 9.0 %collective-permute-start.5 = (bf16[448,128]{1,0:T(8,128)(2,1)S(1)}, bf16[448,128]{1,0:T(8,128)(2,1)S(1)}, u32[]{:S(2)}, u32[]{:S(2)}) collective-permute-start(bf16[448,128]{1,0:T(8,128)(2,1)S(1)} %fusion.6), channel_id=1, source_target_pairs={{0,64},{1,449},{2,66},{3,451},{4,68},{5,453},{6,70},{7,455},{8,72}... | collective-permute-start | bytes 344072 | tf_op jit(solution)/shard_map/ppermute | solution.py:36
  105.0 1.0 copy-start.7
  106.1 12.9 %collective-permute-start.11 = (bf16[448,128]{1,0:T(8,128)(2,1)S(1)}, bf16[448,128]{1,0:T(8,128)(2,1)S(1)}, u32[]{:S(2)}, u32[]{:S(2)}) collective-permute-start(bf16[448,128]{1,0:T(8,128)(2,1)S(1)} %fusion.3), channel_id=1, source_target_pairs={{0,64},{1,449},{2,66},{3,451},{4,68},{5,453},{6,70},{7,455},{8,72}... | collective-permute-start | bytes 344072 | tf_op jit(solution)/shard_map/ppermute | solution.py:36
  108.1 13.5 %collective-permute-start.6 = (bf16[448,128]{1,0:T(8,128)(2,1)S(1)}, bf16[448,128]{1,0:T(8,128)(2,1)S(1)}, u32[]{:S(2)}, u32[]{:S(2)}) collective-permute-start(bf16[448,128]{1,0:T(8,128)(2,1)S(1)} %fusion.5), channel_id=1, source_target_pairs={{0,64},{1,449},{2,66},{3,451},{4,68},{5,453},{6,70},{7,455},{8,72}... | collective-permute-start | bytes 344072 | tf_op jit(solution)/shard_map/ppermute | solution.py:36
  119.1 10.6 %collective-permute-start.12 = (bf16[448,128]{1,0:T(8,128)(2,1)S(1)}, bf16[448,128]{1,0:T(8,128)(2,1)S(1)}, u32[]{:S(2)}, u32[]{:S(2)}) collective-permute-start(bf16[448,128]{1,0:T(8,128)(2,1)S(1)} %fusion.1), channel_id=1, source_target_pairs={{0,64},{1,449},{2,66},{3,451},{4,68},{5,453},{6,70},{7,455},{8,72}... | collective-permute-start | bytes 344072 | tf_op jit(solution)/shard_map/ppermute | solution.py:36
  121.6 11.2 %collective-permute-start.18 = (bf16[464,128]{1,0:T(8,128)(2,1)S(1)}, bf16[464,128]{1,0:T(8,128)(2,1)S(1)}, u32[]{:S(2)}, u32[]{:S(2)}) collective-permute-start(bf16[464,128]{1,0:T(8,128)(2,1)S(1)} %concatenate.11), channel_id=1, source_target_pairs={{0,1},{1,0},{2,3},{3,2},{4,5},{5,4},{6,7},{7,6},{8,9},{9,8},{10,11... | collective-permute-start | bytes 356360 | tf_op jit(solution)/shard_map/ppermute | solution.py:40
  123.9 51.3 %copy-start.2 = (bf16[512,448]{0,1:T(8,128)(2,1)S(1)}, bf16[512,448]{0,1:T(8,128)(2,1)}, u32[]{:S(2)}) copy-start(bf16[512,448]{0,1:T(8,128)(2,1)} %param.13) | copy-start | bytes 1376260
  123.9 51.3 %copy-start.3 = (bf16[512,448]{0,1:T(8,128)(2,1)S(1)}, bf16[512,448]{0,1:T(8,128)(2,1)}, u32[]{:S(2)}) copy-start(bf16[512,448]{0,1:T(8,128)(2,1)} %param.14) | copy-start | bytes 1376260
  129.7 45.6 %copy-start.1 = (bf16[448,2048]{1,0:T(8,128)(2,1)S(1)}, bf16[448,2048]{1,0:T(8,128)(2,1)}, u32[]{:S(2)}) copy-start(bf16[448,2048]{1,0:T(8,128)(2,1)} %get-tuple-element.89.refs_2_.refs_3_) | copy-start | bytes 5505028
  129.7 45.5 %copy-start = (bf16[448,2048]{1,0:T(8,128)(2,1)S(1)}, bf16[448,2048]{1,0:T(8,128)(2,1)}, u32[]{:S(2)}) copy-start(bf16[448,2048]{1,0:T(8,128)(2,1)} %get-tuple-element.88.refs_1_.refs_2_) | copy-start | bytes 5505028
  130.6 7.0 %collective-permute-start.13 = (bf16[464,128]{1,0:T(8,128)(2,1)S(1)}, bf16[464,128]{1,0:T(8,128)(2,1)S(1)}, u32[]{:S(2)}, u32[]{:S(2)}) collective-permute-start(bf16[464,128]{1,0:T(8,128)(2,1)S(1)} %pad_maximum_fusion.4), channel_id=1, source_target_pairs={{0,1},{1,0},{2,3},{3,2},{4,5},{5,4},{6,7},{7,6},{8,9},{9,8},{10,11... | collective-permute-start | bytes 356360 | tf_op jit(solution)/shard_map/ppermute | solution.py:40
  133.5 8.5 %collective-permute-start.19 = (bf16[464,128]{1,0:T(8,128)(2,1)S(1)}, bf16[464,128]{1,0:T(8,128)(2,1)S(1)}, u32[]{:S(2)}, u32[]{:S(2)}) collective-permute-start(bf16[464,128]{1,0:T(8,128)(2,1)S(1)} %add_convert_fusion), channel_id=1, source_target_pairs={{0,64},{1,449},{2,66},{3,451},{4,68},{5,453},{6,70},{7,455},{8,72}... | collective-permute-start | bytes 356360 | tf_op jit(solution)/shard_map/ppermute | solution.py:36
  137.6 7.9 %collective-permute-start.14 = (bf16[464,128]{1,0:T(8,128)(2,1)S(1)}, bf16[464,128]{1,0:T(8,128)(2,1)S(1)}, u32[]{:S(2)}, u32[]{:S(2)}) collective-permute-start(bf16[464,128]{1,0:T(8,128)(2,1)S(1)} %add_convert_fusion.1), channel_id=1, source_target_pairs={{0,64},{1,449},{2,66},{3,451},{4,68},{5,453},{6,70},{7,455},{8,72}... | collective-permute-start | bytes 356360 | tf_op jit(solution)/shard_map/ppermute | solution.py:36
  142.0 8.1 %collective-permute-start.20 = (bf16[464,128]{1,0:T(8,128)(2,1)S(1)}, bf16[464,128]{1,0:T(8,128)(2,1)S(1)}, u32[]{:S(2)}, u32[]{:S(2)}) collective-permute-start(bf16[464,128]{1,0:T(8,128)(2,1)S(1)} %collective-permute-done.19), channel_id=1, source_target_pairs={{0,64},{1,449},{2,66},{3,451},{4,68},{5,453},{6,70},{7,455},{8,72}... | collective-permute-start | bytes 356360 | tf_op jit(solution)/shard_map/ppermute | solution.py:36
  145.5 7.7 %collective-permute-start.15 = (bf16[464,128]{1,0:T(8,128)(2,1)S(1)}, bf16[464,128]{1,0:T(8,128)(2,1)S(1)}, u32[]{:S(2)}, u32[]{:S(2)}) collective-permute-start(bf16[464,128]{1,0:T(8,128)(2,1)S(1)} %collective-permute-done.14), channel_id=1, source_target_pairs={{0,64},{1,449},{2,66},{3,451},{4,68},{5,453},{6,70},{7,455},{8,72}... | collective-permute-start | bytes 356360 | tf_op jit(solution)/shard_map/ppermute | solution.py:36
  150.1 8.6 %collective-permute-start.21 = (bf16[464,128]{1,0:T(8,128)(2,1)S(1)}, bf16[464,128]{1,0:T(8,128)(2,1)S(1)}, u32[]{:S(2)}, u32[]{:S(2)}) collective-permute-start(bf16[464,128]{1,0:T(8,128)(2,1)S(1)} %collective-permute-done.20), channel_id=1, source_target_pairs={{0,64},{1,449},{2,66},{3,451},{4,68},{5,453},{6,70},{7,455},{8,72}... | collective-permute-start | bytes 356360 | tf_op jit(solution)/shard_map/ppermute | solution.py:36
  153.2 11.9 %collective-permute-start.16 = (bf16[464,128]{1,0:T(8,128)(2,1)S(1)}, bf16[464,128]{1,0:T(8,128)(2,1)S(1)}, u32[]{:S(2)}, u32[]{:S(2)}) collective-permute-start(bf16[464,128]{1,0:T(8,128)(2,1)S(1)} %collective-permute-done.15), channel_id=1, source_target_pairs={{0,64},{1,449},{2,66},{3,451},{4,68},{5,453},{6,70},{7,455},{8,72}... | collective-permute-start | bytes 356360 | tf_op jit(solution)/shard_map/ppermute | solution.py:36
  158.7 21.0 %collective-permute-start.22 = (bf16[4,464,128]{2,1,0:T(8,128)(2,1)S(1)}, bf16[4,464,128]{2,1,0:T(8,128)(2,1)S(1)}, u32[]{:S(2)}, u32[]{:S(2)}) collective-permute-start(bf16[4,464,128]{2,1,0:T(8,128)(2,1)S(1)} %pad_maximum_fusion.1.refs_0_), channel_id=1, source_target_pairs={{0,32},{1,481},{2,34},{3,483},{4,36},{5,485},{6,38},{7,487},{8,40}... | collective-permute-start | bytes 1425416 | tf_op jit(solution)/shard_map/ppermute | solution.py:36
  165.2 14.5 %collective-permute-start.17 = (bf16[4,464,128]{2,1,0:T(8,128)(2,1)S(1)}, bf16[4,464,128]{2,1,0:T(8,128)(2,1)S(1)}, u32[]{:S(2)}, u32[]{:S(2)}) collective-permute-start(bf16[4,464,128]{2,1,0:T(8,128)(2,1)S(1)} %pad_maximum_fusion), channel_id=1, source_target_pairs={{0,32},{1,481},{2,34},{3,483},{4,36},{5,485},{6,38},{7,487},{8,40}... | collective-permute-start | bytes 1425416 | tf_op jit(solution)/shard_map/ppermute | solution.py:36
  167.2 9.9 %collective-permute-start.24 = (bf16[3,464,128]{2,1,0:T(8,128)(2,1)S(1)}, bf16[3,464,128]{2,1,0:T(8,128)(2,1)S(1)}, u32[]{:S(2)}, u32[]{:S(2)}) collective-permute-start(bf16[3,464,128]{2,1,0:T(8,128)(2,1)S(1)} %pad_maximum_fusion.2), channel_id=1, source_target_pairs={{0,1},{1,0},{2,3},{3,2},{4,5},{5,4},{6,7},{7,6},{8,9},{9,8},{10,11... | collective-permute-start | bytes 1069064 | tf_op jit(solution)/shard_map/ppermute | solution.py:40
  172.7 7.0 %collective-permute-start.23 = (bf16[464,128]{1,0:T(8,128)(2,1)S(1)}, bf16[464,128]{1,0:T(8,128)(2,1)S(1)}, u32[]{:S(2)}, u32[]{:S(2)}) collective-permute-start(bf16[464,128]{1,0:T(8,128)(2,1)S(1)} %collective-permute-done.21), channel_id=1, source_target_pairs={{0,64},{1,449},{2,66},{3,451},{4,68},{5,453},{6,70},{7,455},{8,72}... | collective-permute-start | bytes 356360 | tf_op jit(solution)/shard_map/ppermute | solution.py:36
  177.1 1.6 copy-start.15
  178.6 0.7 copy-start.21
  179.4 6.2 %copy-start.23 = (bf16[448,384]{1,0:T(8,128)(2,1)}, bf16[448,384]{1,0:T(8,128)(2,1)S(1)}, u32[]{:S(2)}) copy-start(bf16[448,384]{1,0:T(8,128)(2,1)S(1)} %get-tuple-element.119.refs_5_) | copy-start | bytes 1032196
  179.7 9.3 %collective-permute-start.25 = (bf16[4,464,128]{2,1,0:T(8,128)(2,1)S(1)}, bf16[4,464,128]{2,1,0:T(8,128)(2,1)S(1)}, u32[]{:S(2)}, u32[]{:S(2)}) collective-permute-start(bf16[4,464,128]{2,1,0:T(8,128)(2,1)S(1)} %collective-permute-done.17), channel_id=1, source_target_pairs={{0,1},{1,0},{2,3},{3,2},{4,5},{5,4},{6,7},{7,6},{8,9},{9,8},{10,11... | collective-permute-start | bytes 1425416 | tf_op jit(solution)/shard_map/ppermute | solution.py:40
  185.6 0.8 copy-start.17
  186.3 0.8 copy-start.19
  187.1 8.0 %collective-permute-start.26 = (bf16[704,512]{1,0:T(8,128)(2,1)S(1)}, bf16[704,512]{1,0:T(8,128)(2,1)S(1)}, u32[]{:S(2)}, u32[]{:S(2)}) collective-permute-start(bf16[704,512]{1,0:T(8,128)(2,1)S(1)} %get-tuple-element.110), channel_id=1, source_target_pairs={{0,1},{1,0},{2,3},{3,2},{4,5},{5,4},{6,7},{7,6},{8,9},{9,8},{10,11... | collective-permute-start | bytes 2162696 | tf_op jit(solution)/shard_map/ppermute | solution.py:40
  191.1 0.8 copy-start.11
  191.9 0.8 copy-start.13
  192.7 3.7 %collective-permute-start.27 = (bf16[336,512]{1,0:T(8,128)(2,1)S(1)}, bf16[336,512]{1,0:T(8,128)(2,1)S(1)}, u32[]{:S(2)}, u32[]{:S(2)}) collective-permute-start(bf16[336,512]{1,0:T(8,128)(2,1)S(1)} %get-tuple-element.111), channel_id=1, source_target_pairs={{0,1},{1,0},{2,3},{3,2},{4,5},{5,4},{6,7},{7,6},{8,9},{9,8},{10,11... | collective-permute-start | bytes 1032200 | tf_op jit(solution)/shard_map/ppermute | solution.py:40
  198.4 23.4 %all-to-all-start.2 = ((bf16[16,272,128]{2,1,0:T(8,128)(2,1)}), bf16[16,272,128]{2,1,0:T(8,128)(2,1)S(1)}, u32[]{:S(2)}, u32[]{:S(2)}) async-start(bf16[16,272,128]{2,1,0:T(8,128)(2,1)} %merge_cores.1), calls=%async_computation.2 | async-start | bytes 2228224 | tf_op jit(solution)/shard_map/all_to_all | solution.py:45
  204.8 1.2 copy-start.8
  206.0 1.1 copy-start.12
  207.0 1.1 copy-start.14
  208.1 1.0 copy-start.16
  209.1 1.0 copy-start.18
  210.1 1.0 copy-start.20
  211.2 1.0 copy-start.22
  212.1 1.0 copy-start.24
  213.1 8.7 %copy-start.5 = (f32[448,512]{1,0:T(8,128)S(1)}, f32[448,512]{1,0:T(8,128)}, u32[]{:S(2)}) copy-start(f32[448,512]{1,0:T(8,128)} %get-tuple-element.127.update_hbm) | copy-start | bytes 2752516
Sparse Core Ops, SparseCore 0:
  10.7 77.8 all-gather.2
where the time goes:
time: 234 us; the launch traced here: 231 us
  starting transfers between devices  119 us (51%)
  Pallas kernels  29.1 us (12%)
  blocking collectives  22.8 us (10%)
  waiting for transfers between devices  21.5 us (9%)
  local copies, waits for them, and re-layouts  19.6 us (8%)
  between operations  14.8 us (6%)
  other arithmetic  3.88 us (2%)
    ppermute x18, starting transfers between devices, shift_z(): return lax.ppermute(v, ('row', 'col'), pairs)  79.3 us
    ppermute x10, starting transfers between devices, swap_core(): return lax.ppermute(v, 'col', [(c, c ^ 1) for c in range(COLS)])  29.9 us
    all_to_all x1, blocking collectives, exchange_chips(): return lax.all_to_all(v, 'col', 0, 0, axis_index_groups=groups, tiled=True)  22.8 us
    unnamed x56, local copies, waits for them, and re-layouts  17.4 us
    ppermute x18, waiting for transfers between devices, shift_z(): return lax.ppermute(v, ('row', 'col'), pairs)  12.2 us
    all_to_all x2, starting transfers between devices, exchange_chips(): return lax.all_to_all(v, 'col', 0, 0, axis_index_groups=groups, tiled=True)  10 us
    pallas_call x4, Pallas kernels, input_group(): pl.pallas_call(functools.partial(group_body, number, len(grads)), out_sha...  7.09 us
    pallas_call x1, Pallas kernels, down_update(): pl.pallas_call(down_body, out_shape=shapes, in_specs=[HBM] * 5, out_specs...  5.71 us
  transfers between devices with their start and end apart: 31, of which 9 were waited for; matrix products, arithmetic and copies ran while one was open for 2% of the time, Pallas kernels for 11%

commit v1 on v0

--- a/solution.py
+++ b/solution.py
@@ -69,15 +69,16 @@
     for k in (2, 1, 0):
         moving_their = shift_z(moving_their, 2)
         moving = shift_z(moving, 2)
-        moving, ready = lax.optimization_barrier((moving, beside[2 - k]))
-        done.append(ready)
+        if k < 2:
+            moving, ready = lax.optimization_barrier((moving, beside[1 - k]))
+            done.append(ready)
         if k == 2:
             moving = add(moving, even[1], own[2], far)
         elif k == 1:
             moving = add(moving, even[0], own[1])
         if k > 0:
             moving_their = add(moving_their, got_even[k - 1], their[k])
-    extra = done[2]
+    extra = done[1]
     other = jnp.concatenate([add(moving_their, their[0]), jnp.zeros_like(extra)], axis=0)
     mine = jnp.concatenate([add(zero, moving, own[0]), extra], axis=0)
     got_mine = swap_core(other)
@@ -560,8 +561,8 @@
     new_m, new_v, update, sums = down_update(
         hidden, cotangent_all, down_weight, moment_m, moment_v
     )
-    own, other, (tok_other, swish, _) = reduce_z(
-        zero, far, odd, even, give_odd, give_even, (tok_other, swish, sums)
+    own, other, ((swish, tok_other), _) = reduce_z(
+        zero, far, odd, even, give_odd, give_even, ((swish, tok_other), sums)
     )
 
     gate_weight, up_weight = gate_weight.T, up_weight.T

time: 234 us -> 236 us (level)
  starting transfers between devices: 119 us -> 111 us
  waiting for transfers between devices: 21.5 us -> 28.8 us
  other arithmetic: 3.88 us -> 8.57 us
  local copies, waits for them, and re-layouts: 19.6 us -> 17.2 us
    ppermute x18, waiting for transfers between devices: 12.2 us -> 19.5 us  [shift_z(): return lax.ppermute(v, ('row', 'col'), pairs)]
    ppermute x18, starting transfers between devices: 79.3 us -> 73.6 us  [shift_z(): return lax.ppermute(v, ('row', 'col'), pairs)]
    convert_element_type x10, other arithmetic: 1.13 us -> 5.82 us  [add(): return total.astype(BF16)]
    unnamed x56 -> x52, local copies, waits for them, and re-layouts: 17.4 us -> 15.1 us
  transfers between devices with their start and end apart: 31 -> 31, of which waited for: 9 -> 12; matrix products, arithmetic and copies ran while one was open for 2% -> 4% of each run, Pallas kernels for 11% -> 11%
where the time goes in v1:
time: 236 us; the launch traced here: 233 us
  starting transfers between devices  111 us (47%)
  Pallas kernels  29.8 us (13%)
  waiting for transfers between devices  28.8 us (12%)
  blocking collectives  22.8 us (10%)
  local copies, waits for them, and re-layouts  17.2 us (7%)
  between operations  14.7 us (6%)
  other arithmetic  8.57 us (4%)
    ppermute x18, starting transfers between devices, shift_z(): return lax.ppermute(v, ('row', 'col'), pairs)  73.6 us
    ppermute x10, starting transfers between devices, swap_core(): return lax.ppermute(v, 'col', [(c, c ^ 1) for c in range(COLS)])  27.7 us
    all_to_all x1, blocking collectives, exchange_chips(): return lax.all_to_all(v, 'col', 0, 0, axis_index_groups=groups, tiled=True)  22.8 us
    ppermute x18, waiting for transfers between devices, shift_z(): return lax.ppermute(v, ('row', 'col'), pairs)  19.5 us
    unnamed x52, local copies, waits for them, and re-layouts  15.1 us
    all_to_all x2, starting transfers between devices, exchange_chips(): return lax.all_to_all(v, 'col', 0, 0, axis_index_groups=groups, tiled=True)  9.68 us
    pallas_call x4, Pallas kernels, input_group(): pl.pallas_call(functools.partial(group_body, number, len(grads)), out_sha...  7.09 us
    convert_element_type x10, other arithmetic, add(): return total.astype(BF16)  5.82 us
  transfers between devices with their start and end apart: 31, of which 12 were waited for; matrix products, arithmetic and copies ran while one was open for 4% of the time, Pallas kernels for 11%

profile of v1, /device:TPU:1, one launch (start us, length us, event | category | flops | bytes accessed | tf_op | source)
XLA Modules:
  0.0 232.9 jit_solution(16394774198254290124)
XLA Ops:
  7.2 1.7 pad_maximum_fusion.3
  9.9 22.8 %all_to_all.15.mine_ref = bf16[16,64,512]{2,1,0:T(8,128)(2,1)S(1)} all-to-all(bf16[16,64,512]{2,1,0:T(8,128)(2,1)S(1)} %broadcast_in_dim.4), channel_id=1, replica_groups={{0,2,4,6,8,10,12,14,16,18,20,22,24,26,28,30},{1,3,5,7,9,11,13,15,17,19,..., dimensions={0} | all-to-all | bytes 2097152 | tf_op jit(solution)/shard_map/all_to_all | solution.py:45
  32.7 5.0 %collective-permute-start = (bf16[16,64,512]{2,1,0:T(8,128)(2,1)S(1)}, bf16[16,64,512]{2,1,0:T(8,128)(2,1)S(1)}, u32[]{:S(2)}, u32[]{:S(2)}) collective-permute-start(bf16[16,64,512]{2,1,0:T(8,128)(2,1)S(1)} %all_to_all.15.mine_ref), channel_id=1, source_target_pairs={{0,1},{1,0},{2,3},{3,2},{4,5},{5,4},{6,7},{7,6},{8,9},{9,8},{10,11... | collective-permute-start | bytes 3145736 | tf_op jit(solution)/shard_map/ppermute | solution.py:40
  37.8 2.2 collective-permute-done.other_ref
  39.9 1.2 broadcast_in_dim.5
  41.3 3.7 %all-to-all-start.1 = ((bf16[16,64,512]{2,1,0:T(8,128)(2,1)}), bf16[16,64,512]{2,1,0:T(8,128)(2,1)S(1)}, u32[]{:S(2)}, u32[]{:S(2)}) async-start(bf16[16,64,512]{2,1,0:T(8,128)(2,1)} %broadcast_in_dim.5), calls=%async_computation.1 | async-start | bytes 2097152 | tf_op jit(solution)/shard_map/all_to_all | solution.py:45
  44.9 1.2 copy-done.10
  46.2 3.0 %hidden_partial.1 = (bf16[2048,512]{1,0:T(8,128)(2,1)S(1)}, bf16[448,128]{1,0:T(8,128)(2,1)S(1)}, bf16[448,128]{1,0:T(8,128)(2,1)}, bf16[4,448,128]{2,1,0:T(8,12...) custom-call(s32[3]{0:T(128)S(1)} %pad_add_fusion.place_ref, ...), custom_call_target="tpu_custom_call" | custom-call | flops 939524096 | bytes 6488064 | tf_op jit(solution)/shard_map/hidden_partial/pallas_call | solution.py:138
  49.2 1.4 copy-done.4
  50.6 2.3 collective-permute-start.2
  52.9 1.6 collective-permute-done.2
  54.4 10.8 %collective-permute-start.3 = (bf16[4,448,128]{2,1,0:T(8,128)(2,1)}, bf16[4,448,128]{2,1,0:T(8,128)(2,1)}, u32[]{:S(2)}, u32[]{:S(2)}) collective-permute-start(bf16[4,448,128]{2,1,0:T(8,128)(2,1)} %collective-permute-done.2), channel_id=1, source_target_pairs={{0,32},{1,481},{2,34},{3,483},{4,36},{5,485},{6,38},{7,487},{8,40}... | collective-permute-start | bytes 1376264 | tf_op jit(solution)/shard_map/ppermute | solution.py:36
  65.3 1.9 collective-permute-start.1
  67.2 2.6 %collective-permute-start.7 = (bf16[4,448,128]{2,1,0:T(8,128)(2,1)S(1)}, bf16[4,448,128]{2,1,0:T(8,128)(2,1)S(1)}, u32[]{:S(2)}, u32[]{:S(2)}) collective-permute-start(bf16[4,448,128]{2,1,0:T(8,128)(2,1)S(1)} %get-tuple-element.75), channel_id=1, source_target_pairs={{0,32},{1,481},{2,34},{3,483},{4,36},{5,485},{6,38},{7,487},{8,40}... | collective-permute-start | bytes 1376264 | tf_op jit(solution)/shard_map/ppermute | solution.py:36
  69.8 5.8 %collective-permute-start.9 = (bf16[448,128]{1,0:T(8,128)(2,1)}, bf16[448,128]{1,0:T(8,128)(2,1)}, u32[]{:S(2)}, u32[]{:S(2)}) collective-permute-start(bf16[448,128]{1,0:T(8,128)(2,1)} %get-tuple-element.76), channel_id=1, source_target_pairs={{0,128},{1,385},{2,130},{3,387},{4,132},{5,389},{6,134},{7,391},{8... | collective-permute-start | bytes 344072 | tf_op jit(solution)/shard_map/ppermute | solution.py:36
  75.7 1.9 collective-permute-start.11
  78.3 1.0 fusion.7
  79.3 4.2 %collective-permute-start.4 = (bf16[448,128]{1,0:T(8,128)(2,1)S(1)}, bf16[448,128]{1,0:T(8,128)(2,1)S(1)}, u32[]{:S(2)}, u32[]{:S(2)}) collective-permute-start(bf16[448,128]{1,0:T(8,128)(2,1)S(1)} %fusion.7), channel_id=1, source_target_pairs={{0,64},{1,449},{2,66},{3,451},{4,68},{5,453},{6,70},{7,455},{8,72}... | collective-permute-start | bytes 344072 | tf_op jit(solution)/shard_map/ppermute | solution.py:36
  83.5 11.9 %collective-permute-done.7 = bf16[4,448,128]{2,1,0:T(8,128)(2,1)S(1)} collective-permute-done((bf16[4,448,128]{2,1,0:T(8,128)(2,1)S(1)}, bf16[4,448,128]{2,1,0:T(8,128)(2,1)S(1)}, u32[]{:S(2)}, u32[]{:S(2)}) %collective-permute-start.7) | collective-permute-done | bytes 458784 | tf_op jit(solution)/shard_map/ppermute | solution.py:36
  95.4 1.9 collective-permute-start.8
  97.3 1.2 collective-permute-done.4
  98.5 1.0 fusion.6
  99.5 6.0 %collective-permute-start.5 = (bf16[448,128]{1,0:T(8,128)(2,1)S(1)}, bf16[448,128]{1,0:T(8,128)(2,1)S(1)}, u32[]{:S(2)}, u32[]{:S(2)}) collective-permute-start(bf16[448,128]{1,0:T(8,128)(2,1)S(1)} %fusion.6), channel_id=1, source_target_pairs={{0,64},{1,449},{2,66},{3,451},{4,68},{5,453},{6,70},{7,455},{8,72}... | collective-permute-start | bytes 344072 | tf_op jit(solution)/shard_map/ppermute | solution.py:36
  105.5 1.0 fusion.3
  106.5 1.9 collective-permute-start.10
  108.5 1.0 fusion.5
  109.5 5.7 %collective-permute-start.6 = (bf16[448,128]{1,0:T(8,128)(2,1)S(1)}, bf16[448,128]{1,0:T(8,128)(2,1)S(1)}, u32[]{:S(2)}, u32[]{:S(2)}) collective-permute-start(bf16[448,128]{1,0:T(8,128)(2,1)S(1)} %fusion.5), channel_id=1, source_target_pairs={{0,64},{1,449},{2,66},{3,451},{4,68},{5,453},{6,70},{7,455},{8,72}... | collective-permute-start | bytes 344072 | tf_op jit(solution)/shard_map/ppermute | solution.py:36
  115.2 5.3 %activations.1 = (bf16[448,2048]{1,0:T(8,128)(2,1)}, bf16[448,2048]{1,0:T(8,128)(2,1)}, bf16[448,2048]{1,0:T(8,128)(2,1)}) custom-call(bf16[16,896,128]{2,1,0:T(8,128)(2,1)} %bitcast.78), custom_call_target="tpu_custom_call" | custom-call | flops 27525120 | bytes 9175040 | tf_op jit(solution)/shard_map/activations/pallas_call | solution.py:197
  120.6 2.8 %collective-permute-start.12 = (bf16[448,128]{1,0:T(8,128)(2,1)S(1)}, bf16[448,128]{1,0:T(8,128)(2,1)S(1)}, u32[]{:S(2)}, u32[]{:S(2)}) collective-permute-start(bf16[448,128]{1,0:T(8,128)(2,1)S(1)} %fusion.1), channel_id=1, source_target_pairs={{0,64},{1,449},{2,66},{3,451},{4,68},{5,453},{6,70},{7,455},{8,72}... | collective-permute-start | bytes 344072 | tf_op jit(solution)/shard_map/ppermute | solution.py:36
  124.3 1.9 collective-permute-start.18
  126.3 5.7 %down_update.1 = (bf16[448,512]{1,0:T(8,128)(2,1)}, bf16[448,512]{1,0:T(8,128)(2,1)}, f32[448,512]{1,0:T(8,128)}, bf16[16,128]{1,0:T(8,128)(2,1)}) custom-call(bf16[448,2048]{1,0:T(8,128)(2,1)} %get-tuple-element.81.hidden_hbm, bf16[2048,512]{1,0:T(8,128)(2,1)} %copy-done.4, bf16[448,512]{1,0:T(8,128)(2,1)} %weight_hbm.1, bf16[448,512]{1,0:T(8,128)(2,1)} %m_hbm.1, ...), custom_call_target="tpu_custom_call" | custom-call | flops 939524096 | bytes 7143424 | tf_op jit(solution)/shard_map/down_update/pallas_call | solution.py:304
  132.9 2.5 %collective-permute-start.13 = (bf16[464,128]{1,0:T(8,128)(2,1)S(1)}, bf16[464,128]{1,0:T(8,128)(2,1)S(1)}, u32[]{:S(2)}, u32[]{:S(2)}) collective-permute-start(bf16[464,128]{1,0:T(8,128)(2,1)S(1)} %pad_maximum_fusion.4), channel_id=1, source_target_pairs={{0,1},{1,0},{2,3},{3,2},{4,5},{5,4},{6,7},{7,6},{8,9},{9,8},{10,11... | collective-permute-start | bytes 356360 | tf_op jit(solution)/shard_map/ppermute | solution.py:40
  136.2 4.5 %collective-permute-start.19 = (bf16[464,128]{1,0:T(8,128)(2,1)S(1)}, bf16[464,128]{1,0:T(8,128)(2,1)S(1)}, u32[]{:S(2)}, u32[]{:S(2)}) collective-permute-start(bf16[464,128]{1,0:T(8,128)(2,1)S(1)} %add_convert_fusion), channel_id=1, source_target_pairs={{0,64},{1,449},{2,66},{3,451},{4,68},{5,453},{6,70},{7,455},{8,72}... | collective-permute-start | bytes 356360 | tf_op jit(solution)/shard_map/ppermute | solution.py:36
  140.7 1.9 collective-permute-start.14
  142.7 1.1 collective-permute-done.19
  143.7 6.0 %collective-permute-start.20 = (bf16[464,128]{1,0:T(8,128)(2,1)S(1)}, bf16[464,128]{1,0:T(8,128)(2,1)S(1)}, u32[]{:S(2)}, u32[]{:S(2)}) collective-permute-start(bf16[464,128]{1,0:T(8,128)(2,1)S(1)} %collective-permute-done.19), channel_id=1, source_target_pairs={{0,64},{1,449},{2,66},{3,451},{4,68},{5,453},{6,70},{7,455},{8,72}... | collective-permute-start | bytes 356360 | tf_op jit(solution)/shard_map/ppermute | solution.py:36
  149.7 1.9 collective-permute-start.15
  151.7 1.0 collective-permute-done.20
  152.7 6.0 %collective-permute-start.21 = (bf16[464,128]{1,0:T(8,128)(2,1)S(1)}, bf16[464,128]{1,0:T(8,128)(2,1)S(1)}, u32[]{:S(2)}, u32[]{:S(2)}) collective-permute-start(bf16[464,128]{1,0:T(8,128)(2,1)S(1)} %collective-permute-done.20), channel_id=1, source_target_pairs={{0,64},{1,449},{2,66},{3,451},{4,68},{5,453},{6,70},{7,455},{8,72}... | collective-permute-start | bytes 356360 | tf_op jit(solution)/shard_map/ppermute | solution.py:36
  158.8 1.9 collective-permute-start.16
  161.5 3.2 %collective-permute-start.22 = (bf16[4,464,128]{2,1,0:T(8,128)(2,1)S(1)}, bf16[4,464,128]{2,1,0:T(8,128)(2,1)S(1)}, u32[]{:S(2)}, u32[]{:S(2)}) collective-permute-start(bf16[4,464,128]{2,1,0:T(8,128)(2,1)S(1)} %pad_maximum_fusion.1.refs_0_), channel_id=1, source_target_pairs={{0,32},{1,481},{2,34},{3,483},{4,36},{5,485},{6,38},{7,487},{8,40}... | collective-permute-start | bytes 1425416 | tf_op jit(solution)/shard_map/ppermute | solution.py:36
  164.7 2.0 collective-permute-done.16
  166.8 3.9 %collective-permute-start.17 = (bf16[4,464,128]{2,1,0:T(8,128)(2,1)S(1)}, bf16[4,464,128]{2,1,0:T(8,128)(2,1)S(1)}, u32[]{:S(2)}, u32[]{:S(2)}) collective-permute-start(bf16[4,464,128]{2,1,0:T(8,128)(2,1)S(1)} %pad_maximum_fusion), channel_id=1, source_target_pairs={{0,32},{1,481},{2,34},{3,483},{4,36},{5,485},{6,38},{7,487},{8,40}... | collective-permute-start | bytes 1425416 | tf_op jit(solution)/shard_map/ppermute | solution.py:36
  170.8 3.3 %collective-permute-start.24 = (bf16[3,464,128]{2,1,0:T(8,128)(2,1)S(1)}, bf16[3,464,128]{2,1,0:T(8,128)(2,1)S(1)}, u32[]{:S(2)}, u32[]{:S(2)}) collective-permute-start(bf16[3,464,128]{2,1,0:T(8,128)(2,1)S(1)} %pad_maximum_fusion.2), channel_id=1, source_target_pairs={{0,1},{1,0},{2,3},{3,2},{4,5},{5,4},{6,7},{7,6},{8,9},{9,8},{10,11... | collective-permute-start | bytes 1069064 | tf_op jit(solution)/shard_map/ppermute | solution.py:40
  174.1 2.4 %collective-permute-start.23 = (bf16[464,128]{1,0:T(8,128)(2,1)S(1)}, bf16[464,128]{1,0:T(8,128)(2,1)S(1)}, u32[]{:S(2)}, u32[]{:S(2)}) collective-permute-start(bf16[464,128]{1,0:T(8,128)(2,1)S(1)} %collective-permute-done.21), channel_id=1, source_target_pairs={{0,64},{1,449},{2,66},{3,451},{4,68},{5,453},{6,70},{7,455},{8,72}... | collective-permute-start | bytes 356360 | tf_op jit(solution)/shard_map/ppermute | solution.py:36
  176.6 1.8 input_group.4
  178.4 1.5 input_group.5
  181.6 4.5 %collective-permute-start.25 = (bf16[4,464,128]{2,1,0:T(8,128)(2,1)S(1)}, bf16[4,464,128]{2,1,0:T(8,128)(2,1)S(1)}, u32[]{:S(2)}, u32[]{:S(2)}) collective-permute-start(bf16[4,464,128]{2,1,0:T(8,128)(2,1)S(1)} %collective-permute-done.17), channel_id=1, source_target_pairs={{0,1},{1,0},{2,3},{3,2},{4,5},{5,4},{6,7},{7,6},{8,9},{9,8},{10,11... | collective-permute-start | bytes 1425416 | tf_op jit(solution)/shard_map/ppermute | solution.py:40
  186.1 1.8 input_group.6
  189.5 1.9 collective-permute-start.26
  191.4 2.0 input_group.7
  195.1 2.4 %collective-permute-start.27 = (bf16[336,512]{1,0:T(8,128)(2,1)S(1)}, bf16[336,512]{1,0:T(8,128)(2,1)S(1)}, u32[]{:S(2)}, u32[]{:S(2)}) collective-permute-start(bf16[336,512]{1,0:T(8,128)(2,1)S(1)} %get-tuple-element.109), channel_id=1, source_target_pairs={{0,1},{1,0},{2,3},{3,2},{4,5},{5,4},{6,7},{7,6},{8,9},{9,8},{10,11... | collective-permute-start | bytes 1032200 | tf_op jit(solution)/shard_map/ppermute | solution.py:40
  197.5 1.2 collective-permute-done.27.refs_5_
  198.7 2.0 merge_cores.1
  200.8 6.0 %all-to-all-start.2 = ((bf16[16,272,128]{2,1,0:T(8,128)(2,1)}), bf16[16,272,128]{2,1,0:T(8,128)(2,1)S(1)}, u32[]{:S(2)}, u32[]{:S(2)}) async-start(bf16[16,272,128]{2,1,0:T(8,128)(2,1)} %merge_cores.1), calls=%async_computation.2 | async-start | bytes 2228224 | tf_op jit(solution)/shard_map/all_to_all | solution.py:45
  206.8 1.2 copy-done.8
  208.0 1.1 copy-done.12
  209.1 1.1 copy-done.14
  210.2 1.0 copy-done.16
  211.2 1.0 copy-done.18
  212.2 1.0 copy-done.20
  215.2 4.5 %weight_grads.1 = (bf16[448,512]{1,0:T(8,128)(2,1)}, bf16[448,512]{1,0:T(8,128)(2,1)}) custom-call(s32[3]{0:T(128)S(1)} %pad_add_fusion.place_ref, bf16[448,512]{1,0:T(8,128)(2,1)S(1)} %get-tuple-element.112.refs_0_, bf16[448,384]{1,0:T(8,128)(2,1)S(1)} %copy-done.22, bf16[448,512]{1,0:T(8,128)(2,1)S(1)} %copy-done.18, bf16[448,640]{1,0:T(8,128)(2,1)S(1)} %copy-done.12, ...), custom_call_target="tpu_custom_call" | custom-call | flops 1879048192 | bytes 6684672 | tf_op jit(solution)/shard_map/weight_grads/pallas_call | solution.py:528
  219.7 4.2 %all-to-all-done.2.arrived_ref = bf16[16,272,128]{2,1,0:T(8,128)(2,1)S(1)} async-done(((bf16[16,272,128]{2,1,0:T(8,128)(2,1)}), bf16[16,272,128]{2,1,0:T(8,128)(2,1)S(1)}, u32[]{:S(2)}, u32[]{:S(2)}) %all-to-all-start.2) | async-done | bytes 1114144 | tf_op jit(solution)/shard_map/all_to_all | solution.py:45
  223.9 2.2 finish.1
  (81 shorter events, 12.5 us)
Async XLA Ops:
  7.2 108.0 %all-gather.3.cloned.1.call-start = ((), (), s32[]{:S(2)}) async-start(), calls=%async_computation.3 | async-start | bytes 3899392 | tf_op jit(solution)/shard_map/all_gather | solution.py:553
  8.9 31.1 %copy-start.25 = (bf16[64,512]{1,0:T(8,128)(2,1)S(1)}, bf16[64,512]{1,0:T(8,128)(2,1)}, u32[]{:S(2)}) copy-start(bf16[64,512]{1,0:T(8,128)(2,1)} %param.9) | copy-start | bytes 196612
  32.7 12.2 %copy-start.6 = (bf16[448,512]{1,0:T(8,128)(2,1)S(1)}, bf16[448,512]{1,0:T(8,128)(2,1)}, u32[]{:S(2)}) copy-start(bf16[448,512]{1,0:T(8,128)(2,1)} %weight_hbm.1) | copy-start | bytes 1376260
  32.7 7.2 %collective-permute-start = (bf16[16,64,512]{2,1,0:T(8,128)(2,1)S(1)}, bf16[16,64,512]{2,1,0:T(8,128)(2,1)S(1)}, u32[]{:S(2)}, u32[]{:S(2)}) collective-permute-start(bf16[16,64,512]{2,1,0:T(8,128)(2,1)S(1)} %all_to_all.15.mine_ref), channel_id=1, source_target_pairs={{0,1},{1,0},{2,3},{3,2},{4,5},{5,4},{6,7},{7,6},{8,9},{9,8},{10,11... | collective-permute-start | bytes 3145736 | tf_op jit(solution)/shard_map/ppermute | solution.py:40
  39.9 1.3 copy-start.9
  41.3 34.4 %all-to-all-start.1 = ((bf16[16,64,512]{2,1,0:T(8,128)(2,1)}), bf16[16,64,512]{2,1,0:T(8,128)(2,1)S(1)}, u32[]{:S(2)}, u32[]{:S(2)}) async-start(bf16[16,64,512]{2,1,0:T(8,128)(2,1)} %broadcast_in_dim.5), calls=%async_computation.1 | async-start | bytes 2097152 | tf_op jit(solution)/shard_map/all_to_all | solution.py:45
  44.9 1.2 copy-start.10
  49.2 1.4 copy-start.4
  50.6 3.8 %collective-permute-start.2 = (bf16[4,448,128]{2,1,0:T(8,128)(2,1)S(1)}, bf16[4,448,128]{2,1,0:T(8,128)(2,1)}, u32[]{:S(2)}, u32[]{:S(2)}) collective-permute-start(bf16[4,448,128]{2,1,0:T(8,128)(2,1)S(1)} %get-tuple-element.72), channel_id=1, source_target_pairs={{0,1},{1,0},{2,3},{3,2},{4,5},{5,4},{6,7},{7,6},{8,9},{9,8},{10,11... | collective-permute-start | bytes 1376264 | tf_op jit(solution)/shard_map/ppermute | solution.py:40
  54.4 23.9 %collective-permute-start.3 = (bf16[4,448,128]{2,1,0:T(8,128)(2,1)}, bf16[4,448,128]{2,1,0:T(8,128)(2,1)}, u32[]{:S(2)}, u32[]{:S(2)}) collective-permute-start(bf16[4,448,128]{2,1,0:T(8,128)(2,1)} %collective-permute-done.2), channel_id=1, source_target_pairs={{0,32},{1,481},{2,34},{3,483},{4,36},{5,485},{6,38},{7,487},{8,40}... | collective-permute-start | bytes 1376264 | tf_op jit(solution)/shard_map/ppermute | solution.py:36
  65.3 12.4 %collective-permute-start.1 = (bf16[3,448,128]{2,1,0:T(8,128)(2,1)}, bf16[3,448,128]{2,1,0:T(8,128)(2,1)}, u32[]{:S(2)}, u32[]{:S(2)}) collective-permute-start(bf16[3,448,128]{2,1,0:T(8,128)(2,1)} %get-tuple-element.71), channel_id=1, source_target_pairs={{0,1},{1,0},{2,3},{3,2},{4,5},{5,4},{6,7},{7,6},{8,9},{9,8},{10,11... | collective-permute-start | bytes 1032200 | tf_op jit(solution)/shard_map/ppermute | solution.py:40
  67.2 28.2 %collective-permute-start.7 = (bf16[4,448,128]{2,1,0:T(8,128)(2,1)S(1)}, bf16[4,448,128]{2,1,0:T(8,128)(2,1)S(1)}, u32[]{:S(2)}, u32[]{:S(2)}) collective-permute-start(bf16[4,448,128]{2,1,0:T(8,128)(2,1)S(1)} %get-tuple-element.75), channel_id=1, source_target_pairs={{0,32},{1,481},{2,34},{3,483},{4,36},{5,485},{6,38},{7,487},{8,40}... | collective-permute-start | bytes 1376264 | tf_op jit(solution)/shard_map/ppermute | solution.py:36
  69.8 35.7 %collective-permute-start.9 = (bf16[448,128]{1,0:T(8,128)(2,1)}, bf16[448,128]{1,0:T(8,128)(2,1)}, u32[]{:S(2)}, u32[]{:S(2)}) collective-permute-start(bf16[448,128]{1,0:T(8,128)(2,1)} %get-tuple-element.76), channel_id=1, source_target_pairs={{0,128},{1,385},{2,130},{3,387},{4,132},{5,389},{6,134},{7,391},{8... | collective-permute-start | bytes 344072 | tf_op jit(solution)/shard_map/ppermute | solution.py:36
  75.7 44.8 %collective-permute-start.11 = (bf16[16,64,512]{2,1,0:T(8,128)(2,1)S(1)}, bf16[16,64,512]{2,1,0:T(8,128)(2,1)S(1)}, u32[]{:S(2)}, u32[]{:S(2)}) collective-permute-start(bf16[16,64,512]{2,1,0:T(8,128)(2,1)S(1)} %all-to-all-done.1.refs_8_), channel_id=1, source_target_pairs={{0,1},{1,0},{2,3},{3,2},{4,5},{5,4},{6,7},{7,6},{8,9},{9,8},{10,11... | collective-permute-start | bytes 3145736 | tf_op jit(solution)/shard_map/ppermute | solution.py:40
  79.3 19.2 %collective-permute-start.4 = (bf16[448,128]{1,0:T(8,128)(2,1)S(1)}, bf16[448,128]{1,0:T(8,128)(2,1)S(1)}, u32[]{:S(2)}, u32[]{:S(2)}) collective-permute-start(bf16[448,128]{1,0:T(8,128)(2,1)S(1)} %fusion.7), channel_id=1, source_target_pairs={{0,64},{1,449},{2,66},{3,451},{4,68},{5,453},{6,70},{7,455},{8,72}... | collective-permute-start | bytes 344072 | tf_op jit(solution)/shard_map/ppermute | solution.py:36
  95.4 10.1 %collective-permute-start.8 = (bf16[448,128]{1,0:T(8,128)(2,1)S(1)}, bf16[448,128]{1,0:T(8,128)(2,1)S(1)}, u32[]{:S(2)}, u32[]{:S(2)}) collective-permute-start(bf16[448,128]{1,0:T(8,128)(2,1)S(1)} %fusion.8), channel_id=1, source_target_pairs={{0,64},{1,449},{2,66},{3,451},{4,68},{5,453},{6,70},{7,455},{8,72}... | collective-permute-start | bytes 344072 | tf_op jit(solution)/shard_map/ppermute | solution.py:36
  99.5 8.9 %collective-permute-start.5 = (bf16[448,128]{1,0:T(8,128)(2,1)S(1)}, bf16[448,128]{1,0:T(8,128)(2,1)S(1)}, u32[]{:S(2)}, u32[]{:S(2)}) collective-permute-start(bf16[448,128]{1,0:T(8,128)(2,1)S(1)} %fusion.6), channel_id=1, source_target_pairs={{0,64},{1,449},{2,66},{3,451},{4,68},{5,453},{6,70},{7,455},{8,72}... | collective-permute-start | bytes 344072 | tf_op jit(solution)/shard_map/ppermute | solution.py:36
  106.5 14.0 %collective-permute-start.10 = (bf16[448,128]{1,0:T(8,128)(2,1)S(1)}, bf16[448,128]{1,0:T(8,128)(2,1)S(1)}, u32[]{:S(2)}, u32[]{:S(2)}) collective-permute-start(bf16[448,128]{1,0:T(8,128)(2,1)S(1)} %fusion.3), channel_id=1, source_target_pairs={{0,64},{1,449},{2,66},{3,451},{4,68},{5,453},{6,70},{7,455},{8,72}... | collective-permute-start | bytes 344072 | tf_op jit(solution)/shard_map/ppermute | solution.py:36
  109.5 13.9 %collective-permute-start.6 = (bf16[448,128]{1,0:T(8,128)(2,1)S(1)}, bf16[448,128]{1,0:T(8,128)(2,1)S(1)}, u32[]{:S(2)}, u32[]{:S(2)}) collective-permute-start(bf16[448,128]{1,0:T(8,128)(2,1)S(1)} %fusion.5), channel_id=1, source_target_pairs={{0,64},{1,449},{2,66},{3,451},{4,68},{5,453},{6,70},{7,455},{8,72}... | collective-permute-start | bytes 344072 | tf_op jit(solution)/shard_map/ppermute | solution.py:36
  120.5 11.5 %copy-start.7 = (bf16[16,64,512]{2,1,0:T(8,128)(2,1)}, bf16[16,64,512]{2,1,0:T(8,128)(2,1)S(1)}, u32[]{:S(2)}) copy-start(bf16[16,64,512]{2,1,0:T(8,128)(2,1)S(1)} %collective-permute-done.11.refs_9_) | copy-start | bytes 3145732
  120.6 11.5 %collective-permute-start.12 = (bf16[448,128]{1,0:T(8,128)(2,1)S(1)}, bf16[448,128]{1,0:T(8,128)(2,1)S(1)}, u32[]{:S(2)}, u32[]{:S(2)}) collective-permute-start(bf16[448,128]{1,0:T(8,128)(2,1)S(1)} %fusion.1), channel_id=1, source_target_pairs={{0,64},{1,449},{2,66},{3,451},{4,68},{5,453},{6,70},{7,455},{8,72}... | collective-permute-start | bytes 344072 | tf_op jit(solution)/shard_map/ppermute | solution.py:36
  124.3 11.1 %collective-permute-start.18 = (bf16[464,128]{1,0:T(8,128)(2,1)S(1)}, bf16[464,128]{1,0:T(8,128)(2,1)S(1)}, u32[]{:S(2)}, u32[]{:S(2)}) collective-permute-start(bf16[464,128]{1,0:T(8,128)(2,1)S(1)} %concatenate.11), channel_id=1, source_target_pairs={{0,1},{1,0},{2,3},{3,2},{4,5},{5,4},{6,7},{7,6},{8,9},{9,8},{10,11... | collective-permute-start | bytes 356360 | tf_op jit(solution)/shard_map/ppermute | solution.py:40
  126.3 50.3 %copy-start.2 = (bf16[512,448]{0,1:T(8,128)(2,1)S(1)}, bf16[512,448]{0,1:T(8,128)(2,1)}, u32[]{:S(2)}) copy-start(bf16[512,448]{0,1:T(8,128)(2,1)} %param.13) | copy-start | bytes 1376260
  126.3 50.3 %copy-start.3 = (bf16[512,448]{0,1:T(8,128)(2,1)S(1)}, bf16[512,448]{0,1:T(8,128)(2,1)}, u32[]{:S(2)}) copy-start(bf16[512,448]{0,1:T(8,128)(2,1)} %param.14) | copy-start | bytes 1376260
  132.0 44.5 %copy-start.1 = (bf16[448,2048]{1,0:T(8,128)(2,1)S(1)}, bf16[448,2048]{1,0:T(8,128)(2,1)}, u32[]{:S(2)}) copy-start(bf16[448,2048]{1,0:T(8,128)(2,1)} %get-tuple-element.87.refs_2_.refs_3_) | copy-start | bytes 5505028
  132.1 44.5 %copy-start = (bf16[448,2048]{1,0:T(8,128)(2,1)S(1)}, bf16[448,2048]{1,0:T(8,128)(2,1)}, u32[]{:S(2)}) copy-start(bf16[448,2048]{1,0:T(8,128)(2,1)} %get-tuple-element.86.refs_1_.refs_2_) | copy-start | bytes 5505028
  132.9 7.7 %collective-permute-start.13 = (bf16[464,128]{1,0:T(8,128)(2,1)S(1)}, bf16[464,128]{1,0:T(8,128)(2,1)S(1)}, u32[]{:S(2)}, u32[]{:S(2)}) collective-permute-start(bf16[464,128]{1,0:T(8,128)(2,1)S(1)} %pad_maximum_fusion.4), channel_id=1, source_target_pairs={{0,1},{1,0},{2,3},{3,2},{4,5},{5,4},{6,7},{7,6},{8,9},{9,8},{10,11... | collective-permute-start | bytes 356360 | tf_op jit(solution)/shard_map/ppermute | solution.py:40
  136.2 7.5 %collective-permute-start.19 = (bf16[464,128]{1,0:T(8,128)(2,1)S(1)}, bf16[464,128]{1,0:T(8,128)(2,1)S(1)}, u32[]{:S(2)}, u32[]{:S(2)}) collective-permute-start(bf16[464,128]{1,0:T(8,128)(2,1)S(1)} %add_convert_fusion), channel_id=1, source_target_pairs={{0,64},{1,449},{2,66},{3,451},{4,68},{5,453},{6,70},{7,455},{8,72}... | collective-permute-start | bytes 356360 | tf_op jit(solution)/shard_map/ppermute | solution.py:36
  140.7 9.0 %collective-permute-start.14 = (bf16[464,128]{1,0:T(8,128)(2,1)S(1)}, bf16[464,128]{1,0:T(8,128)(2,1)S(1)}, u32[]{:S(2)}, u32[]{:S(2)}) collective-permute-start(bf16[464,128]{1,0:T(8,128)(2,1)S(1)} %add_convert_fusion.1), channel_id=1, source_target_pairs={{0,64},{1,449},{2,66},{3,451},{4,68},{5,453},{6,70},{7,455},{8,72}... | collective-permute-start | bytes 356360 | tf_op jit(solution)/shard_map/ppermute | solution.py:36
  143.7 9.0 %collective-permute-start.20 = (bf16[464,128]{1,0:T(8,128)(2,1)S(1)}, bf16[464,128]{1,0:T(8,128)(2,1)S(1)}, u32[]{:S(2)}, u32[]{:S(2)}) collective-permute-start(bf16[464,128]{1,0:T(8,128)(2,1)S(1)} %collective-permute-done.19), channel_id=1, source_target_pairs={{0,64},{1,449},{2,66},{3,451},{4,68},{5,453},{6,70},{7,455},{8,72}... | collective-permute-start | bytes 356360 | tf_op jit(solution)/shard_map/ppermute | solution.py:36
  149.7 9.0 %collective-permute-start.15 = (bf16[464,128]{1,0:T(8,128)(2,1)S(1)}, bf16[464,128]{1,0:T(8,128)(2,1)S(1)}, u32[]{:S(2)}, u32[]{:S(2)}) collective-permute-start(bf16[464,128]{1,0:T(8,128)(2,1)S(1)} %collective-permute-done.14), channel_id=1, source_target_pairs={{0,64},{1,449},{2,66},{3,451},{4,68},{5,453},{6,70},{7,455},{8,72}... | collective-permute-start | bytes 356360 | tf_op jit(solution)/shard_map/ppermute | solution.py:36
  152.7 8.7 %collective-permute-start.21 = (bf16[464,128]{1,0:T(8,128)(2,1)S(1)}, bf16[464,128]{1,0:T(8,128)(2,1)S(1)}, u32[]{:S(2)}, u32[]{:S(2)}) collective-permute-start(bf16[464,128]{1,0:T(8,128)(2,1)S(1)} %collective-permute-done.20), channel_id=1, source_target_pairs={{0,64},{1,449},{2,66},{3,451},{4,68},{5,453},{6,70},{7,455},{8,72}... | collective-permute-start | bytes 356360 | tf_op jit(solution)/shard_map/ppermute | solution.py:36
  158.8 7.9 %collective-permute-start.16 = (bf16[464,128]{1,0:T(8,128)(2,1)S(1)}, bf16[464,128]{1,0:T(8,128)(2,1)S(1)}, u32[]{:S(2)}, u32[]{:S(2)}) collective-permute-start(bf16[464,128]{1,0:T(8,128)(2,1)S(1)} %collective-permute-done.15), channel_id=1, source_target_pairs={{0,64},{1,449},{2,66},{3,451},{4,68},{5,453},{6,70},{7,455},{8,72}... | collective-permute-start | bytes 356360 | tf_op jit(solution)/shard_map/ppermute | solution.py:36
  161.5 20.1 %collective-permute-start.22 = (bf16[4,464,128]{2,1,0:T(8,128)(2,1)S(1)}, bf16[4,464,128]{2,1,0:T(8,128)(2,1)S(1)}, u32[]{:S(2)}, u32[]{:S(2)}) collective-permute-start(bf16[4,464,128]{2,1,0:T(8,128)(2,1)S(1)} %pad_maximum_fusion.1.refs_0_), channel_id=1, source_target_pairs={{0,32},{1,481},{2,34},{3,483},{4,36},{5,485},{6,38},{7,487},{8,40}... | collective-permute-start | bytes 1425416 | tf_op jit(solution)/shard_map/ppermute | solution.py:36
  166.8 14.8 %collective-permute-start.17 = (bf16[4,464,128]{2,1,0:T(8,128)(2,1)S(1)}, bf16[4,464,128]{2,1,0:T(8,128)(2,1)S(1)}, u32[]{:S(2)}, u32[]{:S(2)}) collective-permute-start(bf16[4,464,128]{2,1,0:T(8,128)(2,1)S(1)} %pad_maximum_fusion), channel_id=1, source_target_pairs={{0,32},{1,481},{2,34},{3,483},{4,36},{5,485},{6,38},{7,487},{8,40}... | collective-permute-start | bytes 1425416 | tf_op jit(solution)/shard_map/ppermute | solution.py:36
  170.8 7.6 %collective-permute-start.24 = (bf16[3,464,128]{2,1,0:T(8,128)(2,1)S(1)}, bf16[3,464,128]{2,1,0:T(8,128)(2,1)S(1)}, u32[]{:S(2)}, u32[]{:S(2)}) collective-permute-start(bf16[3,464,128]{2,1,0:T(8,128)(2,1)S(1)} %pad_maximum_fusion.2), channel_id=1, source_target_pairs={{0,1},{1,0},{2,3},{3,2},{4,5},{5,4},{6,7},{7,6},{8,9},{9,8},{10,11... | collective-permute-start | bytes 1069064 | tf_op jit(solution)/shard_map/ppermute | solution.py:40
  174.1 7.5 %collective-permute-start.23 = (bf16[464,128]{1,0:T(8,128)(2,1)S(1)}, bf16[464,128]{1,0:T(8,128)(2,1)S(1)}, u32[]{:S(2)}, u32[]{:S(2)}) collective-permute-start(bf16[464,128]{1,0:T(8,128)(2,1)S(1)} %collective-permute-done.21), channel_id=1, source_target_pairs={{0,64},{1,449},{2,66},{3,451},{4,68},{5,453},{6,70},{7,455},{8,72}... | collective-permute-start | bytes 356360 | tf_op jit(solution)/shard_map/ppermute | solution.py:36
  178.4 1.6 copy-start.15
  179.9 0.7 copy-start.21
  180.7 7.3 %copy-start.23 = (bf16[448,384]{1,0:T(8,128)(2,1)}, bf16[448,384]{1,0:T(8,128)(2,1)S(1)}, u32[]{:S(2)}) copy-start(bf16[448,384]{1,0:T(8,128)(2,1)S(1)} %get-tuple-element.117.refs_5_) | copy-start | bytes 1032196
  181.6 9.8 %collective-permute-start.25 = (bf16[4,464,128]{2,1,0:T(8,128)(2,1)S(1)}, bf16[4,464,128]{2,1,0:T(8,128)(2,1)S(1)}, u32[]{:S(2)}, u32[]{:S(2)}) collective-permute-start(bf16[4,464,128]{2,1,0:T(8,128)(2,1)S(1)} %collective-permute-done.17), channel_id=1, source_target_pairs={{0,1},{1,0},{2,3},{3,2},{4,5},{5,4},{6,7},{7,6},{8,9},{9,8},{10,11... | collective-permute-start | bytes 1425416 | tf_op jit(solution)/shard_map/ppermute | solution.py:40
  187.9 0.8 copy-start.17
  188.7 0.8 copy-start.19
  189.5 8.0 %collective-permute-start.26 = (bf16[704,512]{1,0:T(8,128)(2,1)S(1)}, bf16[704,512]{1,0:T(8,128)(2,1)S(1)}, u32[]{:S(2)}, u32[]{:S(2)}) collective-permute-start(bf16[704,512]{1,0:T(8,128)(2,1)S(1)} %get-tuple-element.108), channel_id=1, source_target_pairs={{0,1},{1,0},{2,3},{3,2},{4,5},{5,4},{6,7},{7,6},{8,9},{9,8},{10,11... | collective-permute-start | bytes 2162696 | tf_op jit(solution)/shard_map/ppermute | solution.py:40
  193.4 0.8 copy-start.11
  194.3 0.8 copy-start.13
  195.1 3.7 %collective-permute-start.27 = (bf16[336,512]{1,0:T(8,128)(2,1)S(1)}, bf16[336,512]{1,0:T(8,128)(2,1)S(1)}, u32[]{:S(2)}, u32[]{:S(2)}) collective-permute-start(bf16[336,512]{1,0:T(8,128)(2,1)S(1)} %get-tuple-element.109), channel_id=1, source_target_pairs={{0,1},{1,0},{2,3},{3,2},{4,5},{5,4},{6,7},{7,6},{8,9},{9,8},{10,11... | collective-permute-start | bytes 1032200 | tf_op jit(solution)/shard_map/ppermute | solution.py:40
  200.8 23.1 %all-to-all-start.2 = ((bf16[16,272,128]{2,1,0:T(8,128)(2,1)}), bf16[16,272,128]{2,1,0:T(8,128)(2,1)S(1)}, u32[]{:S(2)}, u32[]{:S(2)}) async-start(bf16[16,272,128]{2,1,0:T(8,128)(2,1)} %merge_cores.1), calls=%async_computation.2 | async-start | bytes 2228224 | tf_op jit(solution)/shard_map/all_to_all | solution.py:45
  206.8 1.2 copy-start.8
  208.0 1.1 copy-start.12
  209.1 1.1 copy-start.14
  210.2 1.0 copy-start.16
  211.2 1.0 copy-start.18
  212.2 1.0 copy-start.20
  213.2 1.0 copy-start.22
  214.2 1.0 copy-start.24
  215.2 8.7 %copy-start.5 = (f32[448,512]{1,0:T(8,128)S(1)}, f32[448,512]{1,0:T(8,128)}, u32[]{:S(2)}) copy-start(f32[448,512]{1,0:T(8,128)} %get-tuple-element.125.update_hbm) | copy-start | bytes 2752516
Sparse Core Ops, SparseCore 0:
  10.7 77.8 all-gather.2

commit v2 on v1

--- a/solution.py
+++ b/solution.py
@@ -555,7 +555,7 @@
     cotangent_all, zero, far, odd, even, give_odd, give_even = hidden_partial(
         place, cot_mine, cot_other, down_weight
     )
-    tokens, _ = lax.optimization_barrier((tokens, cot_other))
+    tokens, zero = lax.optimization_barrier((tokens, zero))
     tok_mine, tok_other = gather_chips(tokens)
     swish, slope, hidden = activations(acts)
     new_m, new_v, update, sums = down_update(

time: 236 us -> 236 us (level)
  starting transfers between devices: 111 us -> 116 us
  waiting for transfers between devices: 28.8 us -> 24.6 us
    ppermute x18, waiting for transfers between devices: 19.5 us -> 15.3 us  [shift_z(): return lax.ppermute(v, ('row', 'col'), pairs)]
    ppermute x18, starting transfers between devices: 73.6 us -> 77.5 us  [shift_z(): return lax.ppermute(v, ('row', 'col'), pairs)]
    unnamed x52 -> x54, local copies, waits for them, and re-layouts: 15.1 us -> 14.4 us
  transfers between devices with their start and end apart: 31 -> 31, of which waited for: 12 -> 10; matrix products, arithmetic and copies ran while one was open for 4% -> 4% of each run, Pallas kernels for 11% -> 11%
where the time goes in v2:
time: 236 us; the launch traced here: 234 us
  starting transfers between devices  116 us (49%)
  Pallas kernels  29.8 us (13%)
  waiting for transfers between devices  24.6 us (10%)
  blocking collectives  22.8 us (10%)
  local copies, waits for them, and re-layouts  16.5 us (7%)
  between operations  14.7 us (6%)
  other arithmetic  9.56 us (4%)
    ppermute x18, starting transfers between devices, shift_z(): return lax.ppermute(v, ('row', 'col'), pairs)  77.5 us
    ppermute x10, starting transfers between devices, swap_core(): return lax.ppermute(v, 'col', [(c, c ^ 1) for c in range(COLS)])  29.4 us
    all_to_all x1, blocking collectives, exchange_chips(): return lax.all_to_all(v, 'col', 0, 0, axis_index_groups=groups, tiled=True)  22.8 us
    ppermute x18, waiting for transfers between devices, shift_z(): return lax.ppermute(v, ('row', 'col'), pairs)  15.3 us
    unnamed x54, local copies, waits for them, and re-layouts  14.4 us
    all_to_all x2, starting transfers between devices, exchange_chips(): return lax.all_to_all(v, 'col', 0, 0, axis_index_groups=groups, tiled=True)  9.49 us
    pallas_call x4, Pallas kernels, input_group(): pl.pallas_call(functools.partial(group_body, number, len(grads)), out_sha...  7.12 us
    convert_element_type x10, other arithmetic, add(): return total.astype(BF16)  6.82 us
  transfers between devices with their start and end apart: 31, of which 10 were waited for; matrix products, arithmetic and copies ran while one was open for 4% of the time, Pallas kernels for 11%

profile of v2, /device:TPU:1, one launch (start us, length us, event | category | flops | bytes accessed | tf_op | source)
XLA Modules:
  0.0 234.4 jit_solution(17455829431278714131)
XLA Ops:
  7.2 1.7 pad_maximum_fusion.3
  8.9 1.0 broadcast_in_dim.4
  9.9 22.8 %all_to_all.15.mine_ref = bf16[16,64,512]{2,1,0:T(8,128)(2,1)S(1)} all-to-all(bf16[16,64,512]{2,1,0:T(8,128)(2,1)S(1)} %broadcast_in_dim.4), channel_id=1, replica_groups={{0,2,4,6,8,10,12,14,16,18,20,22,24,26,28,30},{1,3,5,7,9,11,13,15,17,19,..., dimensions={0} | all-to-all | bytes 2097152 | tf_op jit(solution)/shard_map/all_to_all | solution.py:45
  32.7 5.0 %collective-permute-start = (bf16[16,64,512]{2,1,0:T(8,128)(2,1)S(1)}, bf16[16,64,512]{2,1,0:T(8,128)(2,1)S(1)}, u32[]{:S(2)}, u32[]{:S(2)}) collective-permute-start(bf16[16,64,512]{2,1,0:T(8,128)(2,1)S(1)} %all_to_all.15.mine_ref), channel_id=1, source_target_pairs={{0,1},{1,0},{2,3},{3,2},{4,5},{5,4},{6,7},{7,6},{8,9},{9,8},{10,11... | collective-permute-start | bytes 3145736 | tf_op jit(solution)/shard_map/ppermute | solution.py:40
  37.8 2.2 collective-permute-done.other_ref
  40.0 3.1 %hidden_partial.1 = (bf16[2048,512]{1,0:T(8,128)(2,1)S(1)}, bf16[448,128]{1,0:T(8,128)(2,1)S(1)}, bf16[448,128]{1,0:T(8,128)(2,1)}, bf16[4,448,128]{2,1,0:T(8,12...) custom-call(s32[3]{0:T(128)S(1)} %pad_add_fusion.place_ref, ...), custom_call_target="tpu_custom_call" | custom-call | flops 939524096 | bytes 6488064 | tf_op jit(solution)/shard_map/hidden_partial/pallas_call | solution.py:138
  43.0 1.4 copy-done.4
  45.2 1.1 broadcast_in_dim.5
  46.2 3.7 %all-to-all-start.1 = ((bf16[16,64,512]{2,1,0:T(8,128)(2,1)}), bf16[16,64,512]{2,1,0:T(8,128)(2,1)S(1)}, u32[]{:S(2)}, u32[]{:S(2)}) async-start(bf16[16,64,512]{2,1,0:T(8,128)(2,1)} %broadcast_in_dim.5), calls=%async_computation.1 | async-start | bytes 2097152 | tf_op jit(solution)/shard_map/all_to_all | solution.py:45
  49.9 2.3 collective-permute-start.2
  52.2 1.6 collective-permute-done.2
  53.7 10.8 %collective-permute-start.3 = (bf16[4,448,128]{2,1,0:T(8,128)(2,1)}, bf16[4,448,128]{2,1,0:T(8,128)(2,1)}, u32[]{:S(2)}, u32[]{:S(2)}) collective-permute-start(bf16[4,448,128]{2,1,0:T(8,128)(2,1)} %collective-permute-done.2), channel_id=1, source_target_pairs={{0,32},{1,481},{2,34},{3,483},{4,36},{5,485},{6,38},{7,487},{8,40}... | collective-permute-start | bytes 1376264 | tf_op jit(solution)/shard_map/ppermute | solution.py:36
  64.6 1.9 collective-permute-start.1
  66.5 2.6 %collective-permute-start.7 = (bf16[4,448,128]{2,1,0:T(8,128)(2,1)S(1)}, bf16[4,448,128]{2,1,0:T(8,128)(2,1)S(1)}, u32[]{:S(2)}, u32[]{:S(2)}) collective-permute-start(bf16[4,448,128]{2,1,0:T(8,128)(2,1)S(1)} %get-tuple-element.77), channel_id=1, source_target_pairs={{0,32},{1,481},{2,34},{3,483},{4,36},{5,485},{6,38},{7,487},{8,40}... | collective-permute-start | bytes 1376264 | tf_op jit(solution)/shard_map/ppermute | solution.py:36
  69.2 5.8 %collective-permute-start.9 = (bf16[448,128]{1,0:T(8,128)(2,1)}, bf16[448,128]{1,0:T(8,128)(2,1)}, u32[]{:S(2)}, u32[]{:S(2)}) collective-permute-start(bf16[448,128]{1,0:T(8,128)(2,1)} %get-tuple-element.78), channel_id=1, source_target_pairs={{0,128},{1,385},{2,130},{3,387},{4,132},{5,389},{6,134},{7,391},{8... | collective-permute-start | bytes 344072 | tf_op jit(solution)/shard_map/ppermute | solution.py:36
  75.0 1.9 collective-permute-start.11
  77.5 1.0 fusion.7
  78.5 4.8 %collective-permute-start.4 = (bf16[448,128]{1,0:T(8,128)(2,1)S(1)}, bf16[448,128]{1,0:T(8,128)(2,1)S(1)}, u32[]{:S(2)}, u32[]{:S(2)}) collective-permute-start(bf16[448,128]{1,0:T(8,128)(2,1)S(1)} %fusion.7), channel_id=1, source_target_pairs={{0,64},{1,449},{2,66},{3,451},{4,68},{5,453},{6,70},{7,455},{8,72}... | collective-permute-start | bytes 344072 | tf_op jit(solution)/shard_map/ppermute | solution.py:36
  83.3 11.2 %collective-permute-done.7 = bf16[4,448,128]{2,1,0:T(8,128)(2,1)S(1)} collective-permute-done((bf16[4,448,128]{2,1,0:T(8,128)(2,1)S(1)}, bf16[4,448,128]{2,1,0:T(8,128)(2,1)S(1)}, u32[]{:S(2)}, u32[]{:S(2)}) %collective-permute-start.7) | collective-permute-done | bytes 458784 | tf_op jit(solution)/shard_map/ppermute | solution.py:36
  94.6 2.3 collective-permute-start.8
  96.9 1.0 collective-permute-done.4
  97.9 1.0 fusion.6
  98.9 6.0 %collective-permute-start.5 = (bf16[448,128]{1,0:T(8,128)(2,1)S(1)}, bf16[448,128]{1,0:T(8,128)(2,1)S(1)}, u32[]{:S(2)}, u32[]{:S(2)}) collective-permute-start(bf16[448,128]{1,0:T(8,128)(2,1)S(1)} %fusion.6), channel_id=1, source_target_pairs={{0,64},{1,449},{2,66},{3,451},{4,68},{5,453},{6,70},{7,455},{8,72}... | collective-permute-start | bytes 344072 | tf_op jit(solution)/shard_map/ppermute | solution.py:36
  105.9 1.9 collective-permute-start.10
  107.8 1.0 fusion.5
  108.8 5.7 %collective-permute-start.6 = (bf16[448,128]{1,0:T(8,128)(2,1)S(1)}, bf16[448,128]{1,0:T(8,128)(2,1)S(1)}, u32[]{:S(2)}, u32[]{:S(2)}) collective-permute-start(bf16[448,128]{1,0:T(8,128)(2,1)S(1)} %fusion.5), channel_id=1, source_target_pairs={{0,64},{1,449},{2,66},{3,451},{4,68},{5,453},{6,70},{7,455},{8,72}... | collective-permute-start | bytes 344072 | tf_op jit(solution)/shard_map/ppermute | solution.py:36
  114.6 5.2 %activations.1 = (bf16[448,2048]{1,0:T(8,128)(2,1)}, bf16[448,2048]{1,0:T(8,128)(2,1)}, bf16[448,2048]{1,0:T(8,128)(2,1)}) custom-call(bf16[16,896,128]{2,1,0:T(8,128)(2,1)} %bitcast.78), custom_call_target="tpu_custom_call" | custom-call | flops 27525120 | bytes 9175040 | tf_op jit(solution)/shard_map/activations/pallas_call | solution.py:197
  119.9 1.9 collective-permute-start.12
  122.8 3.5 %collective-permute-start.18 = (bf16[464,128]{1,0:T(8,128)(2,1)S(1)}, bf16[464,128]{1,0:T(8,128)(2,1)S(1)}, u32[]{:S(2)}, u32[]{:S(2)}) collective-permute-start(bf16[464,128]{1,0:T(8,128)(2,1)S(1)} %concatenate.11), channel_id=1, source_target_pairs={{0,1},{1,0},{2,3},{3,2},{4,5},{5,4},{6,7},{7,6},{8,9},{9,8},{10,11... | collective-permute-start | bytes 356360 | tf_op jit(solution)/shard_map/ppermute | solution.py:40
  126.3 5.7 %down_update.1 = (bf16[448,512]{1,0:T(8,128)(2,1)}, bf16[448,512]{1,0:T(8,128)(2,1)}, f32[448,512]{1,0:T(8,128)}, bf16[16,128]{1,0:T(8,128)(2,1)}) custom-call(bf16[448,2048]{1,0:T(8,128)(2,1)} %get-tuple-element.83.hidden_hbm, bf16[2048,512]{1,0:T(8,128)(2,1)} %copy-done.4, bf16[448,512]{1,0:T(8,128)(2,1)} %weight_hbm.1, bf16[448,512]{1,0:T(8,128)(2,1)} %m_hbm.1, ...), custom_call_target="tpu_custom_call" | custom-call | flops 939524096 | bytes 7143424 | tf_op jit(solution)/shard_map/down_update/pallas_call | solution.py:304
  132.0 1.1 fusion
  134.0 1.9 collective-permute-start.13
  136.6 4.5 %collective-permute-start.19 = (bf16[464,128]{1,0:T(8,128)(2,1)S(1)}, bf16[464,128]{1,0:T(8,128)(2,1)S(1)}, u32[]{:S(2)}, u32[]{:S(2)}) collective-permute-start(bf16[464,128]{1,0:T(8,128)(2,1)S(1)} %add_convert_fusion), channel_id=1, source_target_pairs={{0,64},{1,449},{2,66},{3,451},{4,68},{5,453},{6,70},{7,455},{8,72}... | collective-permute-start | bytes 356360 | tf_op jit(solution)/shard_map/ppermute | solution.py:36
  141.2 2.4 %collective-permute-start.14 = (bf16[464,128]{1,0:T(8,128)(2,1)S(1)}, bf16[464,128]{1,0:T(8,128)(2,1)S(1)}, u32[]{:S(2)}, u32[]{:S(2)}) collective-permute-start(bf16[464,128]{1,0:T(8,128)(2,1)S(1)} %add_convert_fusion.1), channel_id=1, source_target_pairs={{0,64},{1,449},{2,66},{3,451},{4,68},{5,453},{6,70},{7,455},{8,72}... | collective-permute-start | bytes 356360 | tf_op jit(solution)/shard_map/ppermute | solution.py:36
  144.1 5.9 %collective-permute-start.20 = (bf16[464,128]{1,0:T(8,128)(2,1)S(1)}, bf16[464,128]{1,0:T(8,128)(2,1)S(1)}, u32[]{:S(2)}, u32[]{:S(2)}) collective-permute-start(bf16[464,128]{1,0:T(8,128)(2,1)S(1)} %collective-permute-done.19), channel_id=1, source_target_pairs={{0,64},{1,449},{2,66},{3,451},{4,68},{5,453},{6,70},{7,455},{8,72}... | collective-permute-start | bytes 356360 | tf_op jit(solution)/shard_map/ppermute | solution.py:36
  150.1 1.9 collective-permute-start.15
  152.7 5.9 %collective-permute-start.21 = (bf16[464,128]{1,0:T(8,128)(2,1)S(1)}, bf16[464,128]{1,0:T(8,128)(2,1)S(1)}, u32[]{:S(2)}, u32[]{:S(2)}) collective-permute-start(bf16[464,128]{1,0:T(8,128)(2,1)S(1)} %collective-permute-done.20), channel_id=1, source_target_pairs={{0,64},{1,449},{2,66},{3,451},{4,68},{5,453},{6,70},{7,455},{8,72}... | collective-permute-start | bytes 356360 | tf_op jit(solution)/shard_map/ppermute | solution.py:36
  158.6 1.9 collective-permute-start.16
  160.6 1.2 collective-permute-done.21
  161.8 4.4 %collective-permute-start.22 = (bf16[4,464,128]{2,1,0:T(8,128)(2,1)S(1)}, bf16[4,464,128]{2,1,0:T(8,128)(2,1)S(1)}, u32[]{:S(2)}, u32[]{:S(2)}) collective-permute-start(bf16[4,464,128]{2,1,0:T(8,128)(2,1)S(1)} %pad_maximum_fusion.1.refs_0_), channel_id=1, source_target_pairs={{0,32},{1,481},{2,34},{3,483},{4,36},{5,485},{6,38},{7,487},{8,40}... | collective-permute-start | bytes 1425416 | tf_op jit(solution)/shard_map/ppermute | solution.py:36
  166.3 5.7 %collective-permute-start.17 = (bf16[4,464,128]{2,1,0:T(8,128)(2,1)S(1)}, bf16[4,464,128]{2,1,0:T(8,128)(2,1)S(1)}, u32[]{:S(2)}, u32[]{:S(2)}) collective-permute-start(bf16[4,464,128]{2,1,0:T(8,128)(2,1)S(1)} %pad_maximum_fusion), channel_id=1, source_target_pairs={{0,32},{1,481},{2,34},{3,483},{4,36},{5,485},{6,38},{7,487},{8,40}... | collective-permute-start | bytes 1425416 | tf_op jit(solution)/shard_map/ppermute | solution.py:36
  172.1 4.0 %collective-permute-start.24 = (bf16[3,464,128]{2,1,0:T(8,128)(2,1)S(1)}, bf16[3,464,128]{2,1,0:T(8,128)(2,1)S(1)}, u32[]{:S(2)}, u32[]{:S(2)}) collective-permute-start(bf16[3,464,128]{2,1,0:T(8,128)(2,1)S(1)} %pad_maximum_fusion.2), channel_id=1, source_target_pairs={{0,1},{1,0},{2,3},{3,2},{4,5},{5,4},{6,7},{7,6},{8,9},{9,8},{10,11... | collective-permute-start | bytes 1069064 | tf_op jit(solution)/shard_map/ppermute | solution.py:40
  176.1 2.9 %collective-permute-start.23 = (bf16[464,128]{1,0:T(8,128)(2,1)S(1)}, bf16[464,128]{1,0:T(8,128)(2,1)S(1)}, u32[]{:S(2)}, u32[]{:S(2)}) collective-permute-start(bf16[464,128]{1,0:T(8,128)(2,1)S(1)} %collective-permute-done.21), channel_id=1, source_target_pairs={{0,64},{1,449},{2,66},{3,451},{4,68},{5,453},{6,70},{7,455},{8,72}... | collective-permute-start | bytes 356360 | tf_op jit(solution)/shard_map/ppermute | solution.py:36
  179.1 1.8 input_group.4
  180.9 1.5 input_group.5
  183.2 4.7 %collective-permute-start.25 = (bf16[4,464,128]{2,1,0:T(8,128)(2,1)S(1)}, bf16[4,464,128]{2,1,0:T(8,128)(2,1)S(1)}, u32[]{:S(2)}, u32[]{:S(2)}) collective-permute-start(bf16[4,464,128]{2,1,0:T(8,128)(2,1)S(1)} %collective-permute-done.17), channel_id=1, source_target_pairs={{0,1},{1,0},{2,3},{3,2},{4,5},{5,4},{6,7},{7,6},{8,9},{9,8},{10,11... | collective-permute-start | bytes 1425416 | tf_op jit(solution)/shard_map/ppermute | solution.py:40
  187.8 1.8 input_group.6
  191.2 1.9 collective-permute-start.26
  193.1 2.0 input_group.7
  196.8 2.4 %collective-permute-start.27 = (bf16[336,512]{1,0:T(8,128)(2,1)S(1)}, bf16[336,512]{1,0:T(8,128)(2,1)S(1)}, u32[]{:S(2)}, u32[]{:S(2)}) collective-permute-start(bf16[336,512]{1,0:T(8,128)(2,1)S(1)} %get-tuple-element.111), channel_id=1, source_target_pairs={{0,1},{1,0},{2,3},{3,2},{4,5},{5,4},{6,7},{7,6},{8,9},{9,8},{10,11... | collective-permute-start | bytes 1032200 | tf_op jit(solution)/shard_map/ppermute | solution.py:40
  199.2 1.2 collective-permute-done.27.refs_5_
  200.5 2.0 merge_cores.1
  202.5 5.8 %all-to-all-start.2 = ((bf16[16,272,128]{2,1,0:T(8,128)(2,1)}), bf16[16,272,128]{2,1,0:T(8,128)(2,1)S(1)}, u32[]{:S(2)}, u32[]{:S(2)}) async-start(bf16[16,272,128]{2,1,0:T(8,128)(2,1)} %merge_cores.1), calls=%async_computation.2 | async-start | bytes 2228224 | tf_op jit(solution)/shard_map/all_to_all | solution.py:45
  208.4 1.2 copy-done.8
  209.6 1.1 copy-done.10
  210.6 1.1 copy-done.12
  211.7 1.0 copy-done.14
  212.7 1.0 copy-done.16
  213.7 1.0 copy-done.18
  214.7 1.0 copy-done.22
  215.7 1.0 copy-done.24
  216.7 4.5 %weight_grads.1 = (bf16[448,512]{1,0:T(8,128)(2,1)}, bf16[448,512]{1,0:T(8,128)(2,1)}) custom-call(s32[3]{0:T(128)S(1)} %pad_add_fusion.place_ref, bf16[448,512]{1,0:T(8,128)(2,1)S(1)} %get-tuple-element.114.refs_0_, bf16[448,384]{1,0:T(8,128)(2,1)S(1)} %copy-done.22, bf16[448,512]{1,0:T(8,128)(2,1)S(1)} %copy-done.16, bf16[448,640]{1,0:T(8,128)(2,1)S(1)} %copy-done.10, ...), custom_call_target="tpu_custom_call" | custom-call | flops 1879048192 | bytes 6684672 | tf_op jit(solution)/shard_map/weight_grads/pallas_call | solution.py:528
  221.2 4.2 %all-to-all-done.2.arrived_ref = bf16[16,272,128]{2,1,0:T(8,128)(2,1)S(1)} async-done(((bf16[16,272,128]{2,1,0:T(8,128)(2,1)}), bf16[16,272,128]{2,1,0:T(8,128)(2,1)S(1)}, u32[]{:S(2)}, u32[]{:S(2)}) %all-to-all-start.2) | async-done | bytes 1114144 | tf_op jit(solution)/shard_map/all_to_all | solution.py:45
  225.4 2.2 finish.1
  (83 shorter events, 10.5 us)
Async XLA Ops:
  7.2 107.4 %all-gather.3.cloned.1.call-start = ((), (), s32[]{:S(2)}) async-start(), calls=%async_computation.3 | async-start | bytes 3899392 | tf_op jit(solution)/shard_map/all_gather | solution.py:553
  8.9 31.1 %copy-start.6 = (bf16[448,512]{1,0:T(8,128)(2,1)S(1)}, bf16[448,512]{1,0:T(8,128)(2,1)}, u32[]{:S(2)}) copy-start(bf16[448,512]{1,0:T(8,128)(2,1)} %weight_hbm.1) | copy-start | bytes 1376260
  32.7 12.4 %copy-start.26 = (bf16[64,512]{1,0:T(8,128)(2,1)S(1)}, bf16[64,512]{1,0:T(8,128)(2,1)}, u32[]{:S(2)}) copy-start(bf16[64,512]{1,0:T(8,128)(2,1)} %param.9) | copy-start | bytes 196612
  32.7 7.2 %collective-permute-start = (bf16[16,64,512]{2,1,0:T(8,128)(2,1)S(1)}, bf16[16,64,512]{2,1,0:T(8,128)(2,1)S(1)}, u32[]{:S(2)}, u32[]{:S(2)}) collective-permute-start(bf16[16,64,512]{2,1,0:T(8,128)(2,1)S(1)} %all_to_all.15.mine_ref), channel_id=1, source_target_pairs={{0,1},{1,0},{2,3},{3,2},{4,5},{5,4},{6,7},{7,6},{8,9},{9,8},{10,11... | collective-permute-start | bytes 3145736 | tf_op jit(solution)/shard_map/ppermute | solution.py:40
  43.0 1.4 copy-start.4
  44.4 0.8 copy-start.19
  45.2 4.7 %copy-start.20 = (bf16[4,448,128]{2,1,0:T(8,128)(2,1)S(1)}, bf16[4,448,128]{2,1,0:T(8,128)(2,1)}, u32[]{:S(2)}) copy-start(bf16[4,448,128]{2,1,0:T(8,128)(2,1)} %copy-done.19) | copy-start | bytes 1376260
  46.2 28.8 %all-to-all-start.1 = ((bf16[16,64,512]{2,1,0:T(8,128)(2,1)}), bf16[16,64,512]{2,1,0:T(8,128)(2,1)S(1)}, u32[]{:S(2)}, u32[]{:S(2)}) async-start(bf16[16,64,512]{2,1,0:T(8,128)(2,1)} %broadcast_in_dim.5), calls=%async_computation.1 | async-start | bytes 2097152 | tf_op jit(solution)/shard_map/all_to_all | solution.py:45
  49.9 3.8 %collective-permute-start.2 = (bf16[4,448,128]{2,1,0:T(8,128)(2,1)S(1)}, bf16[4,448,128]{2,1,0:T(8,128)(2,1)}, u32[]{:S(2)}, u32[]{:S(2)}) collective-permute-start(bf16[4,448,128]{2,1,0:T(8,128)(2,1)S(1)} %copy-done.20), channel_id=1, source_target_pairs={{0,1},{1,0},{2,3},{3,2},{4,5},{5,4},{6,7},{7,6},{8,9},{9,8},{10,11... | collective-permute-start | bytes 1376264 | tf_op jit(solution)/shard_map/ppermute | solution.py:40
  53.7 23.7 %collective-permute-start.3 = (bf16[4,448,128]{2,1,0:T(8,128)(2,1)}, bf16[4,448,128]{2,1,0:T(8,128)(2,1)}, u32[]{:S(2)}, u32[]{:S(2)}) collective-permute-start(bf16[4,448,128]{2,1,0:T(8,128)(2,1)} %collective-permute-done.2), channel_id=1, source_target_pairs={{0,32},{1,481},{2,34},{3,483},{4,36},{5,485},{6,38},{7,487},{8,40}... | collective-permute-start | bytes 1376264 | tf_op jit(solution)/shard_map/ppermute | solution.py:36
  64.6 12.4 %collective-permute-start.1 = (bf16[3,448,128]{2,1,0:T(8,128)(2,1)}, bf16[3,448,128]{2,1,0:T(8,128)(2,1)}, u32[]{:S(2)}, u32[]{:S(2)}) collective-permute-start(bf16[3,448,128]{2,1,0:T(8,128)(2,1)} %get-tuple-element.72), channel_id=1, source_target_pairs={{0,1},{1,0},{2,3},{3,2},{4,5},{5,4},{6,7},{7,6},{8,9},{9,8},{10,11... | collective-permute-start | bytes 1032200 | tf_op jit(solution)/shard_map/ppermute | solution.py:40
  66.5 28.0 %collective-permute-start.7 = (bf16[4,448,128]{2,1,0:T(8,128)(2,1)S(1)}, bf16[4,448,128]{2,1,0:T(8,128)(2,1)S(1)}, u32[]{:S(2)}, u32[]{:S(2)}) collective-permute-start(bf16[4,448,128]{2,1,0:T(8,128)(2,1)S(1)} %get-tuple-element.77), channel_id=1, source_target_pairs={{0,32},{1,481},{2,34},{3,483},{4,36},{5,485},{6,38},{7,487},{8,40}... | collective-permute-start | bytes 1376264 | tf_op jit(solution)/shard_map/ppermute | solution.py:36
  69.2 35.7 %collective-permute-start.9 = (bf16[448,128]{1,0:T(8,128)(2,1)}, bf16[448,128]{1,0:T(8,128)(2,1)}, u32[]{:S(2)}, u32[]{:S(2)}) collective-permute-start(bf16[448,128]{1,0:T(8,128)(2,1)} %get-tuple-element.78), channel_id=1, source_target_pairs={{0,128},{1,385},{2,130},{3,387},{4,132},{5,389},{6,134},{7,391},{8... | collective-permute-start | bytes 344072 | tf_op jit(solution)/shard_map/ppermute | solution.py:36
  75.0 44.8 %collective-permute-start.11 = (bf16[16,64,512]{2,1,0:T(8,128)(2,1)S(1)}, bf16[16,64,512]{2,1,0:T(8,128)(2,1)S(1)}, u32[]{:S(2)}, u32[]{:S(2)}) collective-permute-start(bf16[16,64,512]{2,1,0:T(8,128)(2,1)S(1)} %all-to-all-done.1.refs_8_), channel_id=1, source_target_pairs={{0,1},{1,0},{2,3},{3,2},{4,5},{5,4},{6,7},{7,6},{8,9},{9,8},{10,11... | collective-permute-start | bytes 3145736 | tf_op jit(solution)/shard_map/ppermute | solution.py:40
  78.5 19.5 %collective-permute-start.4 = (bf16[448,128]{1,0:T(8,128)(2,1)S(1)}, bf16[448,128]{1,0:T(8,128)(2,1)S(1)}, u32[]{:S(2)}, u32[]{:S(2)}) collective-permute-start(bf16[448,128]{1,0:T(8,128)(2,1)S(1)} %fusion.7), channel_id=1, source_target_pairs={{0,64},{1,449},{2,66},{3,451},{4,68},{5,453},{6,70},{7,455},{8,72}... | collective-permute-start | bytes 344072 | tf_op jit(solution)/shard_map/ppermute | solution.py:36
  94.5 25.3 %copy-start.25 = (bf16[4,448,128]{2,1,0:T(8,128)(2,1)}, bf16[4,448,128]{2,1,0:T(8,128)(2,1)S(1)}, u32[]{:S(2)}) copy-start(bf16[4,448,128]{2,1,0:T(8,128)(2,1)S(1)} %collective-permute-done.7) | copy-start | bytes 1376260
  94.6 10.3 %collective-permute-start.8 = (bf16[448,128]{1,0:T(8,128)(2,1)S(1)}, bf16[448,128]{1,0:T(8,128)(2,1)S(1)}, u32[]{:S(2)}, u32[]{:S(2)}) collective-permute-start(bf16[448,128]{1,0:T(8,128)(2,1)S(1)} %fusion.8), channel_id=1, source_target_pairs={{0,64},{1,449},{2,66},{3,451},{4,68},{5,453},{6,70},{7,455},{8,72}... | collective-permute-start | bytes 344072 | tf_op jit(solution)/shard_map/ppermute | solution.py:36
  98.9 8.9 %collective-permute-start.5 = (bf16[448,128]{1,0:T(8,128)(2,1)S(1)}, bf16[448,128]{1,0:T(8,128)(2,1)S(1)}, u32[]{:S(2)}, u32[]{:S(2)}) collective-permute-start(bf16[448,128]{1,0:T(8,128)(2,1)S(1)} %fusion.6), channel_id=1, source_target_pairs={{0,64},{1,449},{2,66},{3,451},{4,68},{5,453},{6,70},{7,455},{8,72}... | collective-permute-start | bytes 344072 | tf_op jit(solution)/shard_map/ppermute | solution.py:36
  105.9 13.9 %collective-permute-start.10 = (bf16[448,128]{1,0:T(8,128)(2,1)S(1)}, bf16[448,128]{1,0:T(8,128)(2,1)S(1)}, u32[]{:S(2)}, u32[]{:S(2)}) collective-permute-start(bf16[448,128]{1,0:T(8,128)(2,1)S(1)} %fusion.3), channel_id=1, source_target_pairs={{0,64},{1,449},{2,66},{3,451},{4,68},{5,453},{6,70},{7,455},{8,72}... | collective-permute-start | bytes 344072 | tf_op jit(solution)/shard_map/ppermute | solution.py:36
  108.8 13.0 %collective-permute-start.6 = (bf16[448,128]{1,0:T(8,128)(2,1)S(1)}, bf16[448,128]{1,0:T(8,128)(2,1)S(1)}, u32[]{:S(2)}, u32[]{:S(2)}) collective-permute-start(bf16[448,128]{1,0:T(8,128)(2,1)S(1)} %fusion.5), channel_id=1, source_target_pairs={{0,64},{1,449},{2,66},{3,451},{4,68},{5,453},{6,70},{7,455},{8,72}... | collective-permute-start | bytes 344072 | tf_op jit(solution)/shard_map/ppermute | solution.py:36
  119.8 12.2 %copy-start.7 = (bf16[16,64,512]{2,1,0:T(8,128)(2,1)}, bf16[16,64,512]{2,1,0:T(8,128)(2,1)S(1)}, u32[]{:S(2)}) copy-start(bf16[16,64,512]{2,1,0:T(8,128)(2,1)S(1)} %collective-permute-done.11.refs_9_) | copy-start | bytes 3145732
  119.9 12.1 %collective-permute-start.12 = (bf16[448,128]{1,0:T(8,128)(2,1)S(1)}, bf16[448,128]{1,0:T(8,128)(2,1)S(1)}, u32[]{:S(2)}, u32[]{:S(2)}) collective-permute-start(bf16[448,128]{1,0:T(8,128)(2,1)S(1)} %fusion.1), channel_id=1, source_target_pairs={{0,64},{1,449},{2,66},{3,451},{4,68},{5,453},{6,70},{7,455},{8,72}... | collective-permute-start | bytes 344072 | tf_op jit(solution)/shard_map/ppermute | solution.py:36
  122.8 13.1 %collective-permute-start.18 = (bf16[464,128]{1,0:T(8,128)(2,1)S(1)}, bf16[464,128]{1,0:T(8,128)(2,1)S(1)}, u32[]{:S(2)}, u32[]{:S(2)}) collective-permute-start(bf16[464,128]{1,0:T(8,128)(2,1)S(1)} %concatenate.11), channel_id=1, source_target_pairs={{0,1},{1,0},{2,3},{3,2},{4,5},{5,4},{6,7},{7,6},{8,9},{9,8},{10,11... | collective-permute-start | bytes 356360 | tf_op jit(solution)/shard_map/ppermute | solution.py:40
  126.3 52.7 %copy-start.2 = (bf16[512,448]{0,1:T(8,128)(2,1)S(1)}, bf16[512,448]{0,1:T(8,128)(2,1)}, u32[]{:S(2)}) copy-start(bf16[512,448]{0,1:T(8,128)(2,1)} %param.13) | copy-start | bytes 1376260
  126.3 52.7 %copy-start.3 = (bf16[512,448]{0,1:T(8,128)(2,1)S(1)}, bf16[512,448]{0,1:T(8,128)(2,1)}, u32[]{:S(2)}) copy-start(bf16[512,448]{0,1:T(8,128)(2,1)} %param.14) | copy-start | bytes 1376260
  132.0 47.0 %copy-start.1 = (bf16[448,2048]{1,0:T(8,128)(2,1)S(1)}, bf16[448,2048]{1,0:T(8,128)(2,1)}, u32[]{:S(2)}) copy-start(bf16[448,2048]{1,0:T(8,128)(2,1)} %get-tuple-element.89.refs_2_.refs_3_) | copy-start | bytes 5505028
  133.1 45.9 %copy-start = (bf16[448,2048]{1,0:T(8,128)(2,1)S(1)}, bf16[448,2048]{1,0:T(8,128)(2,1)}, u32[]{:S(2)}) copy-start(bf16[448,2048]{1,0:T(8,128)(2,1)} %get-tuple-element.88.refs_1_.refs_2_) | copy-start | bytes 5505028
  134.0 7.2 %collective-permute-start.13 = (bf16[464,128]{1,0:T(8,128)(2,1)S(1)}, bf16[464,128]{1,0:T(8,128)(2,1)S(1)}, u32[]{:S(2)}, u32[]{:S(2)}) collective-permute-start(bf16[464,128]{1,0:T(8,128)(2,1)S(1)} %pad_maximum_fusion.4), channel_id=1, source_target_pairs={{0,1},{1,0},{2,3},{3,2},{4,5},{5,4},{6,7},{7,6},{8,9},{9,8},{10,11... | collective-permute-start | bytes 356360 | tf_op jit(solution)/shard_map/ppermute | solution.py:40
  136.6 7.5 %collective-permute-start.19 = (bf16[464,128]{1,0:T(8,128)(2,1)S(1)}, bf16[464,128]{1,0:T(8,128)(2,1)S(1)}, u32[]{:S(2)}, u32[]{:S(2)}) collective-permute-start(bf16[464,128]{1,0:T(8,128)(2,1)S(1)} %add_convert_fusion), channel_id=1, source_target_pairs={{0,64},{1,449},{2,66},{3,451},{4,68},{5,453},{6,70},{7,455},{8,72}... | collective-permute-start | bytes 356360 | tf_op jit(solution)/shard_map/ppermute | solution.py:36
  141.2 8.9 %collective-permute-start.14 = (bf16[464,128]{1,0:T(8,128)(2,1)S(1)}, bf16[464,128]{1,0:T(8,128)(2,1)S(1)}, u32[]{:S(2)}, u32[]{:S(2)}) collective-permute-start(bf16[464,128]{1,0:T(8,128)(2,1)S(1)} %add_convert_fusion.1), channel_id=1, source_target_pairs={{0,64},{1,449},{2,66},{3,451},{4,68},{5,453},{6,70},{7,455},{8,72}... | collective-permute-start | bytes 356360 | tf_op jit(solution)/shard_map/ppermute | solution.py:36
  144.1 8.6 %collective-permute-start.20 = (bf16[464,128]{1,0:T(8,128)(2,1)S(1)}, bf16[464,128]{1,0:T(8,128)(2,1)S(1)}, u32[]{:S(2)}, u32[]{:S(2)}) collective-permute-start(bf16[464,128]{1,0:T(8,128)(2,1)S(1)} %collective-permute-done.19), channel_id=1, source_target_pairs={{0,64},{1,449},{2,66},{3,451},{4,68},{5,453},{6,70},{7,455},{8,72}... | collective-permute-start | bytes 356360 | tf_op jit(solution)/shard_map/ppermute | solution.py:36
  150.1 8.6 %collective-permute-start.15 = (bf16[464,128]{1,0:T(8,128)(2,1)S(1)}, bf16[464,128]{1,0:T(8,128)(2,1)S(1)}, u32[]{:S(2)}, u32[]{:S(2)}) collective-permute-start(bf16[464,128]{1,0:T(8,128)(2,1)S(1)} %collective-permute-done.14), channel_id=1, source_target_pairs={{0,64},{1,449},{2,66},{3,451},{4,68},{5,453},{6,70},{7,455},{8,72}... | collective-permute-start | bytes 356360 | tf_op jit(solution)/shard_map/ppermute | solution.py:36
  152.7 9.0 %collective-permute-start.21 = (bf16[464,128]{1,0:T(8,128)(2,1)S(1)}, bf16[464,128]{1,0:T(8,128)(2,1)S(1)}, u32[]{:S(2)}, u32[]{:S(2)}) collective-permute-start(bf16[464,128]{1,0:T(8,128)(2,1)S(1)} %collective-permute-done.20), channel_id=1, source_target_pairs={{0,64},{1,449},{2,66},{3,451},{4,68},{5,453},{6,70},{7,455},{8,72}... | collective-permute-start | bytes 356360 | tf_op jit(solution)/shard_map/ppermute | solution.py:36
  158.6 7.6 %collective-permute-start.16 = (bf16[464,128]{1,0:T(8,128)(2,1)S(1)}, bf16[464,128]{1,0:T(8,128)(2,1)S(1)}, u32[]{:S(2)}, u32[]{:S(2)}) collective-permute-start(bf16[464,128]{1,0:T(8,128)(2,1)S(1)} %collective-permute-done.15), channel_id=1, source_target_pairs={{0,64},{1,449},{2,66},{3,451},{4,68},{5,453},{6,70},{7,455},{8,72}... | collective-permute-start | bytes 356360 | tf_op jit(solution)/shard_map/ppermute | solution.py:36
  161.8 21.3 %collective-permute-start.22 = (bf16[4,464,128]{2,1,0:T(8,128)(2,1)S(1)}, bf16[4,464,128]{2,1,0:T(8,128)(2,1)S(1)}, u32[]{:S(2)}, u32[]{:S(2)}) collective-permute-start(bf16[4,464,128]{2,1,0:T(8,128)(2,1)S(1)} %pad_maximum_fusion.1.refs_0_), channel_id=1, source_target_pairs={{0,32},{1,481},{2,34},{3,483},{4,36},{5,485},{6,38},{7,487},{8,40}... | collective-permute-start | bytes 1425416 | tf_op jit(solution)/shard_map/ppermute | solution.py:36
  166.3 16.8 %collective-permute-start.17 = (bf16[4,464,128]{2,1,0:T(8,128)(2,1)S(1)}, bf16[4,464,128]{2,1,0:T(8,128)(2,1)S(1)}, u32[]{:S(2)}, u32[]{:S(2)}) collective-permute-start(bf16[4,464,128]{2,1,0:T(8,128)(2,1)S(1)} %pad_maximum_fusion), channel_id=1, source_target_pairs={{0,32},{1,481},{2,34},{3,483},{4,36},{5,485},{6,38},{7,487},{8,40}... | collective-permute-start | bytes 1425416 | tf_op jit(solution)/shard_map/ppermute | solution.py:36
  172.1 8.8 %collective-permute-start.24 = (bf16[3,464,128]{2,1,0:T(8,128)(2,1)S(1)}, bf16[3,464,128]{2,1,0:T(8,128)(2,1)S(1)}, u32[]{:S(2)}, u32[]{:S(2)}) collective-permute-start(bf16[3,464,128]{2,1,0:T(8,128)(2,1)S(1)} %pad_maximum_fusion.2), channel_id=1, source_target_pairs={{0,1},{1,0},{2,3},{3,2},{4,5},{5,4},{6,7},{7,6},{8,9},{9,8},{10,11... | collective-permute-start | bytes 1069064 | tf_op jit(solution)/shard_map/ppermute | solution.py:40
  176.1 7.1 %collective-permute-start.23 = (bf16[464,128]{1,0:T(8,128)(2,1)S(1)}, bf16[464,128]{1,0:T(8,128)(2,1)S(1)}, u32[]{:S(2)}, u32[]{:S(2)}) collective-permute-start(bf16[464,128]{1,0:T(8,128)(2,1)S(1)} %collective-permute-done.21), channel_id=1, source_target_pairs={{0,64},{1,449},{2,66},{3,451},{4,68},{5,453},{6,70},{7,455},{8,72}... | collective-permute-start | bytes 356360 | tf_op jit(solution)/shard_map/ppermute | solution.py:36
  180.8 1.6 copy-start.13
  182.4 0.7 copy-start.21
  183.1 6.5 %copy-start.23 = (bf16[448,384]{1,0:T(8,128)(2,1)}, bf16[448,384]{1,0:T(8,128)(2,1)S(1)}, u32[]{:S(2)}) copy-start(bf16[448,384]{1,0:T(8,128)(2,1)S(1)} %get-tuple-element.119.refs_5_) | copy-start | bytes 1032196
  183.2 9.9 %collective-permute-start.25 = (bf16[4,464,128]{2,1,0:T(8,128)(2,1)S(1)}, bf16[4,464,128]{2,1,0:T(8,128)(2,1)S(1)}, u32[]{:S(2)}, u32[]{:S(2)}) collective-permute-start(bf16[4,464,128]{2,1,0:T(8,128)(2,1)S(1)} %collective-permute-done.17), channel_id=1, source_target_pairs={{0,1},{1,0},{2,3},{3,2},{4,5},{5,4},{6,7},{7,6},{8,9},{9,8},{10,11... | collective-permute-start | bytes 1425416 | tf_op jit(solution)/shard_map/ppermute | solution.py:40
  189.6 0.8 copy-start.15
  190.4 0.8 copy-start.17
  191.2 8.0 %collective-permute-start.26 = (bf16[704,512]{1,0:T(8,128)(2,1)S(1)}, bf16[704,512]{1,0:T(8,128)(2,1)S(1)}, u32[]{:S(2)}, u32[]{:S(2)}) collective-permute-start(bf16[704,512]{1,0:T(8,128)(2,1)S(1)} %get-tuple-element.110), channel_id=1, source_target_pairs={{0,1},{1,0},{2,3},{3,2},{4,5},{5,4},{6,7},{7,6},{8,9},{9,8},{10,11... | collective-permute-start | bytes 2162696 | tf_op jit(solution)/shard_map/ppermute | solution.py:40
  195.2 0.8 copy-start.9
  196.0 0.8 copy-start.11
  196.8 3.7 %collective-permute-start.27 = (bf16[336,512]{1,0:T(8,128)(2,1)S(1)}, bf16[336,512]{1,0:T(8,128)(2,1)S(1)}, u32[]{:S(2)}, u32[]{:S(2)}) collective-permute-start(bf16[336,512]{1,0:T(8,128)(2,1)S(1)} %get-tuple-element.111), channel_id=1, source_target_pairs={{0,1},{1,0},{2,3},{3,2},{4,5},{5,4},{6,7},{7,6},{8,9},{9,8},{10,11... | collective-permute-start | bytes 1032200 | tf_op jit(solution)/shard_map/ppermute | solution.py:40
  202.5 22.9 %all-to-all-start.2 = ((bf16[16,272,128]{2,1,0:T(8,128)(2,1)}), bf16[16,272,128]{2,1,0:T(8,128)(2,1)S(1)}, u32[]{:S(2)}, u32[]{:S(2)}) async-start(bf16[16,272,128]{2,1,0:T(8,128)(2,1)} %merge_cores.1), calls=%async_computation.2 | async-start | bytes 2228224 | tf_op jit(solution)/shard_map/all_to_all | solution.py:45
  208.3 1.2 copy-start.8
  209.6 1.1 copy-start.10
  210.6 1.1 copy-start.12
  211.7 1.0 copy-start.14
  212.7 1.0 copy-start.16
  213.7 1.0 copy-start.18
  214.7 1.0 copy-start.22
  215.7 1.0 copy-start.24
  216.7 8.7 %copy-start.5 = (f32[448,512]{1,0:T(8,128)S(1)}, f32[448,512]{1,0:T(8,128)}, u32[]{:S(2)}) copy-start(f32[448,512]{1,0:T(8,128)} %get-tuple-element.127.update_hbm) | copy-start | bytes 2752516
Sparse Core Ops, SparseCore 0:
  10.7 79.5 all-gather.2
